TPU v7x, 32 devices: a whole 2x2x4 slice. The times are simulated.
32 devices in a mesh: seq: 4 (over y, core), dp: 8 (over z, x).
Axes of the slice: x: 2, y: 2, z: 4, core: 2. Of those that a mesh axis runs over, the one named last changes fastest.
Arguments:
- tokens: bfloat16 [16, 1024, 1024], P('dp', 'seq'), may hold values from -6 to 6
- lengths: int32 [16], P('dp'), may hold values from 256 to 1024, as said below
- cotangent: bfloat16 [16, 1024, 1024], P('dp', 'seq'), may hold values from -6 to 6
- first_gain: bfloat16 [1024], P(('seq', 'dp')), may hold values from 0.5 to 1.5
- first_bias: bfloat16 [1024], P(('seq', 'dp')), may hold values from -1 to 1
- mix_key: bfloat16 [1024], P(('seq', 'dp')), may hold values from 0 to 1
- mix_value: bfloat16 [1024], P(('seq', 'dp')), may hold values from 0 to 1
- mix_recept: bfloat16 [1024], P(('seq', 'dp')), may hold values from 0 to 1
- time_decay: bfloat16 [1024], P(('seq', 'dp')), as said below
- time_first: bfloat16 [1024], P(('seq', 'dp')), may hold values from -1 to 1
- key_weight: bfloat16 [1024, 1024], P(('seq', 'dp')), may hold values from -0.1875 to 0.1875
- value_weight: bfloat16 [1024, 1024], P(('seq', 'dp')), may hold values from -0.1875 to 0.1875
- recept_weight: bfloat16 [1024, 1024], P(('seq', 'dp')), may hold values from -0.1875 to 0.1875
- output_weight: bfloat16 [1024, 1024], P(('seq', 'dp')), may hold values from -0.75 to 0.75
- second_gain: bfloat16 [1024], P(('seq', 'dp')), may hold values from 0.5 to 1.5
- second_bias: bfloat16 [1024], P(('seq', 'dp')), may hold values from -1 to 1
- shift_key: bfloat16 [1024], P(('seq', 'dp')), may hold values from 0 to 1
- shift_recept: bfloat16 [1024], P(('seq', 'dp')), may hold values from 0 to 1
- up_weight: bfloat16 [1024, 4096], P(('seq', 'dp')), may hold values from -0.1875 to 0.1875
- gate_weight: bfloat16 [1024, 1024], P(('seq', 'dp')), may hold values from -0.1875 to 0.1875
- down_weight: bfloat16 [4096, 1024], P(('seq', 'dp')), may hold values from -0.09375 to 0.09375
Outputs:
- output: bfloat16 [16, 1024, 1024], P('dp', 'seq')
- tokens_grad: float32 [16, 1024, 1024], P('dp', 'seq')
- grad_first_gain: float32 [1024], P(('seq', 'dp'))
- grad_first_bias: float32 [1024], P(('seq', 'dp'))
- grad_mix_key: float32 [1024], P(('seq', 'dp'))
- grad_mix_value: float32 [1024], P(('seq', 'dp'))
- grad_mix_recept: float32 [1024], P(('seq', 'dp'))
- grad_time_decay: float32 [1024], P(('seq', 'dp'))
- grad_time_first: float32 [1024], P(('seq', 'dp'))
- grad_key_weight: float32 [1024, 1024], P(('seq', 'dp'))
- grad_value_weight: float32 [1024, 1024], P(('seq', 'dp'))
- grad_recept_weight: float32 [1024, 1024], P(('seq', 'dp'))
- grad_output_weight: float32 [1024, 1024], P(('seq', 'dp'))
- grad_second_gain: float32 [1024], P(('seq', 'dp'))
- grad_second_bias: float32 [1024], P(('seq', 'dp'))
- grad_shift_key: float32 [1024], P(('seq', 'dp'))
- grad_shift_recept: float32 [1024], P(('seq', 'dp'))
- grad_up_weight: float32 [1024, 4096], P(('seq', 'dp'))
- grad_gate_weight: float32 [1024, 1024], P(('seq', 'dp'))
- grad_down_weight: float32 [4096, 1024], P(('seq', 'dp'))
Inputs may be any that keep to these rules, and one draw needn't show every extreme that they name: `lengths`: each sequence has between 256 and 1024 live tokens at its start, the rest of its slots are padding; some sequence has each of the two. exp(time_decay) lies between 0.3 / 1024 and 0.08.
All inputs are finite; a program needn't handle non-finite values.
Results may differ from a plain program's by a relative error of at most 0.013.
Values may be sent and summed in bfloat16 or wider, within the bound.
No kernel may reach another device: no remote copies, remote signals or barrier semaphores. Data moves between devices by JAX's collectives and lax.ppermute only.
A program may use at most 256 MiB of HBM per device.

v0:
```python
import jax
import jax.numpy as jnp
from jax import lax
from jax.sharding import PartitionSpec as P

BLK = 64


EPS = 1e-05


def shifted(block, axis, distance):
    devices = range(lax.axis_size(axis))
    route = [(i - distance, i) for i in devices if i - distance in devices]
    return lax.ppermute(block, axis, route)


def prefix(x, axis, combine, identity, reverse):
    count, mine = (lax.axis_size(axis), lax.axis_index(axis))
    everything = jax.tree.map(lambda part: lax.all_gather(part, axis), x)
    start = jax.tree.map(
        lambda part, zero: jnp.broadcast_to(jnp.asarray(zero, part.dtype), part.shape), x, identity
    )

    def step(k, before):
        at = count - 1 - k if reverse else k
        reached = at > mine if reverse else at < mine
        new = combine(before, jax.tree.map(lambda part: part[at], everything))
        return jax.tree.map(lambda a, b: jnp.where(reached, a, b), new, before)

    return lax.fori_loop(0, count, step, start)


def norm_stats(field):
    center = field - jnp.mean(field, axis=-1, keepdims=True)
    inverse = lax.rsqrt(jnp.mean(center * center, axis=-1, keepdims=True) + EPS)
    return (center * inverse, inverse)


def norm_back(grad_normed, normalized, inverse):
    mean_grad = jnp.mean(grad_normed, axis=-1, keepdims=True)
    mean_proj = jnp.mean(grad_normed * normalized, axis=-1, keepdims=True)
    return inverse * (grad_normed - mean_grad - normalized * mean_proj)


def previous_rows(field):
    came = shifted(field[:, -1, :], "seq", 1)
    return jnp.concatenate([came[:, None, :], field[:, :-1, :]], axis=1)


def next_rows(field):
    came = shifted(field[:, 0, :], "seq", -1)
    return jnp.concatenate([field[:, 1:, :], came[:, None, :]], axis=1)


def summary(lookup_matrix_output, content_matrix_output, fading_rate_vector):
    span_len = lookup_matrix_output.shape[1]
    distance = (span_len - 1 - jnp.arange(span_len, dtype=jnp.float32))[:, None]
    weight = jnp.exp(lookup_matrix_output - distance * fading_rate_vector)
    return (jnp.sum(weight * content_matrix_output, axis=1), jnp.sum(weight, axis=1))


def combine_state(earlier, later):
    return (
        earlier[0] * later[0],
        later[0] * earlier[1] + later[1],
        later[0] * earlier[2] + later[2],
    )


def compute_attention_recurrence(
    lookup_matrix_output,
    content_matrix_output,
    fading_rate_vector,
    boost_log_scale,
    starting_accumulator,
    starting_normalizer,
):
    seq_count, span_len, channels = lookup_matrix_output.shape
    blocks = span_len // BLK
    offset = jnp.arange(BLK, dtype=jnp.float32)[:, None]
    strict_lower = (jnp.arange(BLK)[:, None] > jnp.arange(BLK)[None, :]).astype(jnp.float32)
    rising = jnp.exp(offset * fading_rate_vector)
    falling = jnp.exp(-offset * fading_rate_vector)
    carry_fall = jnp.exp((1.0 - offset) * fading_rate_vector)
    end_fall = jnp.exp(-BLK * fading_rate_vector)
    end_carry = jnp.exp((1.0 - BLK) * fading_rate_vector)

    def one_block(state, inputs):
        state_a, state_b = state
        lookup_piece_entries, content_piece_entries = inputs
        weight = jnp.exp(lookup_piece_entries) * rising
        weighted = weight * content_piece_entries
        sum_a = jnp.einsum("ts,nsc->ntc", strict_lower, weighted, precision=lax.Precision.HIGHEST)
        sum_b = jnp.einsum("ts,nsc->ntc", strict_lower, weight, precision=lax.Precision.HIGHEST)
        earlier_accumulator = falling * state_a[:, None, :] + carry_fall * sum_a
        earlier_normalizer = falling * state_b[:, None, :] + carry_fall * sum_b
        current_token_boost = jnp.exp(boost_log_scale + lookup_piece_entries)
        module_output_tensor = (
            earlier_accumulator + current_token_boost * content_piece_entries
        ) / (earlier_normalizer + current_token_boost)
        next_a = end_fall * state_a + end_carry * jnp.sum(weighted, axis=1)
        next_b = end_fall * state_b + end_carry * jnp.sum(weight, axis=1)
        return ((next_a, next_b), module_output_tensor)

    key_seq = jnp.moveaxis(lookup_matrix_output.reshape(seq_count, blocks, BLK, channels), 1, 0)
    value_seq = jnp.moveaxis(content_matrix_output.reshape(seq_count, blocks, BLK, channels), 1, 0)
    final_state, results = lax.scan(
        jax.checkpoint(one_block), (starting_accumulator, starting_normalizer), (key_seq, value_seq)
    )
    return jnp.moveaxis(results, 0, 1).reshape(seq_count, span_len, channels)


def unpack(gathered):
    return tuple(
        (element.astype(jnp.float32) if element.ndim == 1 else element for element in gathered)
    )


def matmul(form, left, right):
    return jnp.einsum(form, left, right, preferred_element_type=jnp.float32)


def per_device(
    tokens,
    lengths,
    cotangent,
    first_gain,
    first_bias,
    mix_key,
    mix_value,
    mix_recept,
    time_decay,
    time_first,
    key_weight,
    value_weight,
    recept_weight,
    output_weight,
    second_gain,
    second_bias,
    shift_key,
    shift_recept,
    up_weight,
    gate_weight,
    down_weight,
):
    shards = (
        first_gain,
        first_bias,
        mix_key,
        mix_value,
        mix_recept,
        time_decay,
        time_first,
        key_weight,
        value_weight,
        recept_weight,
        output_weight,
        second_gain,
        second_bias,
        shift_key,
        shift_recept,
        up_weight,
        gate_weight,
        down_weight,
    )
    gathered = (
        lax.all_gather(shards[0], ("seq", "dp"), axis=0, tiled=True),
        lax.all_gather(shards[1], ("seq", "dp"), axis=0, tiled=True),
        lax.all_gather(shards[2], ("seq", "dp"), axis=0, tiled=True),
        lax.all_gather(shards[3], ("seq", "dp"), axis=0, tiled=True),
        lax.all_gather(shards[4], ("seq", "dp"), axis=0, tiled=True),
        lax.all_gather(shards[5], ("seq", "dp"), axis=0, tiled=True),
        lax.all_gather(shards[6], ("seq", "dp"), axis=0, tiled=True),
        lax.all_gather(shards[7], ("seq", "dp"), axis=0, tiled=True),
        lax.all_gather(shards[8], ("seq", "dp"), axis=0, tiled=True),
        lax.all_gather(shards[9], ("seq", "dp"), axis=0, tiled=True),
        lax.all_gather(shards[10], ("seq", "dp"), axis=0, tiled=True),
        lax.all_gather(shards[11], ("seq", "dp"), axis=0, tiled=True),
        lax.all_gather(shards[12], ("seq", "dp"), axis=0, tiled=True),
        lax.all_gather(shards[13], ("seq", "dp"), axis=0, tiled=True),
        lax.all_gather(shards[14], ("seq", "dp"), axis=0, tiled=True),
        lax.all_gather(shards[15], ("seq", "dp"), axis=0, tiled=True),
        lax.all_gather(shards[16], ("seq", "dp"), axis=0, tiled=True),
        lax.all_gather(shards[17], ("seq", "dp"), axis=0, tiled=True),
    )
    (
        norm_gain,
        norm_bias,
        key_mix,
        value_mix,
        recept_mix,
        decay_log,
        boost_log_scale,
        key_mat,
        value_mat,
        recept_mat,
        output_mat,
        gain_two,
        bias_two,
        chan_key_mix,
        chan_recept_mix,
        up_mat,
        gate_mat,
        down_mat,
    ) = unpack(gathered)
    seq_index = lax.axis_index("seq")
    seq_count, piece_len, channels = tokens.shape
    positions = seq_index * piece_len + jnp.arange(piece_len, dtype=jnp.int32)
    live_mask = (positions[None, :] < lengths[:, None]).astype(jnp.float32)[:, :, None]
    field = tokens.astype(jnp.float32)
    normed_one, inverse_one = norm_stats(field)
    normed = normed_one * norm_gain + norm_bias
    before = previous_rows(normed)
    key_in = (normed * key_mix + before * (1.0 - key_mix)).astype(jnp.bfloat16)
    value_in = (normed * value_mix + before * (1.0 - value_mix)).astype(jnp.bfloat16)
    recept_in = (normed * recept_mix + before * (1.0 - recept_mix)).astype(jnp.bfloat16)
    lookup_matrix_output = matmul("nlc,cd->nld", key_in, key_mat)
    content_matrix_output = matmul("nlc,cd->nld", value_in, value_mat)
    recept_proj = matmul("nlc,cd->nld", recept_in, recept_mat)
    fading_rate_vector = jnp.exp(decay_log)
    (local_a, local_b), summary_pull = jax.vjp(
        summary, lookup_matrix_output, content_matrix_output, fading_rate_vector
    )
    piece_fall = jnp.exp(-piece_len * fading_rate_vector)
    factor = jnp.broadcast_to(piece_fall, local_a.shape)
    identity = (jnp.ones_like(local_a), jnp.zeros_like(local_a), jnp.zeros_like(local_a))
    scanned = prefix((factor, local_a, local_b), "seq", combine_state, identity, False)
    starting_accumulator, starting_normalizer = (scanned[1], scanned[2])
    blended, weighted_kv_pullback = jax.vjp(
        compute_attention_recurrence,
        lookup_matrix_output,
        content_matrix_output,
        fading_rate_vector,
        boost_log_scale,
        starting_accumulator,
        starting_normalizer,
    )
    recept_sig = jax.nn.sigmoid(recept_proj)
    mixed_out = (recept_sig * blended).astype(jnp.bfloat16)
    branch = matmul("nlc,cd->nld", mixed_out, output_mat)
    residual = field + branch
    normed_two_raw, inverse_two = norm_stats(residual)
    normed_two = normed_two_raw * gain_two + bias_two
    before_two = previous_rows(normed_two)
    ffn_key = (normed_two * chan_key_mix + before_two * (1.0 - chan_key_mix)).astype(jnp.bfloat16)
    ffn_recept = (normed_two * chan_recept_mix + before_two * (1.0 - chan_recept_mix)).astype(
        jnp.bfloat16
    )
    up_proj = matmul("nlc,cf->nlf", ffn_key, up_mat)
    squared = jnp.square(jax.nn.relu(up_proj)).astype(jnp.bfloat16)
    down_proj = matmul("nlf,fd->nld", squared, down_mat)
    gate_value = jax.nn.sigmoid(matmul("nlc,cd->nld", ffn_recept, gate_mat))
    output = ((residual + gate_value * down_proj) * live_mask).astype(jnp.bfloat16)
    regathered = (
        lax.all_gather(shards[0], ("seq", "dp"), axis=0, tiled=True),
        lax.all_gather(shards[1], ("seq", "dp"), axis=0, tiled=True),
        lax.all_gather(shards[2], ("seq", "dp"), axis=0, tiled=True),
        lax.all_gather(shards[3], ("seq", "dp"), axis=0, tiled=True),
        lax.all_gather(shards[4], ("seq", "dp"), axis=0, tiled=True),
        lax.all_gather(shards[5], ("seq", "dp"), axis=0, tiled=True),
        lax.all_gather(shards[6], ("seq", "dp"), axis=0, tiled=True),
        lax.all_gather(shards[7], ("seq", "dp"), axis=0, tiled=True),
        lax.all_gather(shards[8], ("seq", "dp"), axis=0, tiled=True),
        lax.all_gather(shards[9], ("seq", "dp"), axis=0, tiled=True),
        lax.all_gather(shards[10], ("seq", "dp"), axis=0, tiled=True),
        lax.all_gather(shards[11], ("seq", "dp"), axis=0, tiled=True),
        lax.all_gather(shards[12], ("seq", "dp"), axis=0, tiled=True),
        lax.all_gather(shards[13], ("seq", "dp"), axis=0, tiled=True),
        lax.all_gather(shards[14], ("seq", "dp"), axis=0, tiled=True),
        lax.all_gather(shards[15], ("seq", "dp"), axis=0, tiled=True),
        lax.all_gather(shards[16], ("seq", "dp"), axis=0, tiled=True),
        lax.all_gather(shards[17], ("seq", "dp"), axis=0, tiled=True),
    )
    (
        norm_gain,
        norm_bias,
        key_mix,
        value_mix,
        recept_mix,
        decay_log,
        boost_log_scale,
        key_mat,
        value_mat,
        recept_mat,
        output_mat,
        gain_two,
        bias_two,
        chan_key_mix,
        chan_recept_mix,
        up_mat,
        gate_mat,
        down_mat,
    ) = unpack(regathered)
    seed = cotangent.astype(jnp.float32) * live_mask
    down_grad = (seed * gate_value).astype(jnp.bfloat16)
    gate_grad = (seed * down_proj * gate_value * (1.0 - gate_value)).astype(jnp.bfloat16)
    rows_in = squared
    grad_down = lax.psum_scatter(
        matmul("nlf,nld->fd", rows_in, down_grad), ("seq", "dp"), scatter_dimension=0, tiled=True
    )
    rows_in = ffn_recept
    grad_gate = lax.psum_scatter(
        matmul("nlc,nld->cd", rows_in, gate_grad), ("seq", "dp"), scatter_dimension=0, tiled=True
    )
    squared_grad = matmul("nld,fd->nlf", down_grad, down_mat)
    up_grad = (squared_grad * 2.0 * jax.nn.relu(up_proj)).astype(jnp.bfloat16)
    rows_in = ffn_key
    grad_up = lax.psum_scatter(
        matmul("nlc,nlf->cf", rows_in, up_grad), ("seq", "dp"), scatter_dimension=0, tiled=True
    )
    ffn_key_grad = matmul("nlf,cf->nlc", up_grad, up_mat)
    ffn_recept_grad = matmul("nld,cd->nlc", gate_grad, gate_mat)
    normed_two_grad = (
        ffn_key_grad * chan_key_mix
        + ffn_recept_grad * chan_recept_mix
        + next_rows(ffn_key_grad * (1.0 - chan_key_mix) + ffn_recept_grad * (1.0 - chan_recept_mix))
    )
    gap_two = normed_two - before_two
    grad_chan_key = jnp.sum(ffn_key_grad * gap_two, axis=(0, 1))
    grad_chan_recept = jnp.sum(ffn_recept_grad * gap_two, axis=(0, 1))
    grad_gain_two = jnp.sum(normed_two_grad * normed_two_raw, axis=(0, 1))
    grad_bias_two = jnp.sum(normed_two_grad, axis=(0, 1))
    residual_grad = seed + norm_back(normed_two_grad * gain_two, normed_two_raw, inverse_two)
    branch_grad = residual_grad.astype(jnp.bfloat16)
    grad_output = matmul("nlc,nld->cd", mixed_out, branch_grad)
    mixed_grad = matmul("nld,cd->nlc", branch_grad, output_mat)
    recept_grad = (mixed_grad * blended * recept_sig * (1.0 - recept_sig)).astype(jnp.bfloat16)
    blended_grad = mixed_grad * recept_sig
    (
        key_gradient_first,
        value_gradient_first,
        decay_gradient_first,
        boost_adjoint_term,
        initial_numerator_gradient,
        initial_denominator_gradient,
    ) = weighted_kv_pullback(blended_grad)
    identity_back = (jnp.ones_like(local_a), jnp.zeros_like(local_a), jnp.zeros_like(local_a))
    carried = prefix(
        (factor, initial_numerator_gradient, initial_denominator_gradient),
        "seq",
        combine_state,
        identity_back,
        True,
    )
    carry_a, carry_b = (carried[1], carried[2])
    key_grad_b, value_grad_b, rate_grad_b = summary_pull((carry_a, carry_b))
    factor_grad = jnp.sum(carry_a * starting_accumulator + carry_b * starting_normalizer, axis=0)
    rate_grad = decay_gradient_first + rate_grad_b - piece_len * piece_fall * factor_grad
    grad_decay = rate_grad * fading_rate_vector
    key_grad = (key_gradient_first + key_grad_b).astype(jnp.bfloat16)
    value_grad = (value_gradient_first + value_grad_b).astype(jnp.bfloat16)
    grad_key = matmul("nlc,nld->cd", key_in, key_grad)
    grad_value = matmul("nlc,nld->cd", value_in, value_grad)
    grad_recept = matmul("nlc,nld->cd", recept_in, recept_grad)
    key_in_grad = matmul("nld,cd->nlc", key_grad, key_mat)
    value_in_grad = matmul("nld,cd->nlc", value_grad, value_mat)
    recept_in_grad = matmul("nld,cd->nlc", recept_grad, recept_mat)
    normed_grad = (
        key_in_grad * key_mix
        + value_in_grad * value_mix
        + recept_in_grad * recept_mix
        + next_rows(
            key_in_grad * (1.0 - key_mix)
            + value_in_grad * (1.0 - value_mix)
            + recept_in_grad * (1.0 - recept_mix)
        )
    )
    gap_one = normed - before
    grad_key_mix = jnp.sum(key_in_grad * gap_one, axis=(0, 1))
    grad_value_mix = jnp.sum(value_in_grad * gap_one, axis=(0, 1))
    grad_recept_mix = jnp.sum(recept_in_grad * gap_one, axis=(0, 1))
    grad_gain_one = jnp.sum(normed_grad * normed_one, axis=(0, 1))
    grad_bias_one = jnp.sum(normed_grad, axis=(0, 1))
    tokens_grad = residual_grad + norm_back(normed_grad * norm_gain, normed_one, inverse_one)
    summed = (
        lax.psum_scatter(grad_gain_one, ("seq", "dp"), scatter_dimension=0, tiled=True),
        lax.psum_scatter(grad_bias_one, ("seq", "dp"), scatter_dimension=0, tiled=True),
        lax.psum_scatter(grad_key_mix, ("seq", "dp"), scatter_dimension=0, tiled=True),
        lax.psum_scatter(grad_value_mix, ("seq", "dp"), scatter_dimension=0, tiled=True),
        lax.psum_scatter(grad_recept_mix, ("seq", "dp"), scatter_dimension=0, tiled=True),
        lax.psum_scatter(grad_decay, ("seq", "dp"), scatter_dimension=0, tiled=True),
        lax.psum_scatter(boost_adjoint_term, ("seq", "dp"), scatter_dimension=0, tiled=True),
        lax.psum_scatter(grad_key, ("seq", "dp"), scatter_dimension=0, tiled=True),
        lax.psum_scatter(grad_value, ("seq", "dp"), scatter_dimension=0, tiled=True),
        lax.psum_scatter(grad_recept, ("seq", "dp"), scatter_dimension=0, tiled=True),
        lax.psum_scatter(grad_output, ("seq", "dp"), scatter_dimension=0, tiled=True),
        lax.psum_scatter(grad_gain_two, ("seq", "dp"), scatter_dimension=0, tiled=True),
        lax.psum_scatter(grad_bias_two, ("seq", "dp"), scatter_dimension=0, tiled=True),
        lax.psum_scatter(grad_chan_key, ("seq", "dp"), scatter_dimension=0, tiled=True),
        lax.psum_scatter(grad_chan_recept, ("seq", "dp"), scatter_dimension=0, tiled=True),
    )
    return (output, tokens_grad) + tuple(summed) + (grad_up, grad_gate, grad_down)


def solution(mesh):
    placed = (
        P("dp", "seq", None),
        P("dp"),
        P("dp", "seq", None),
        P(("seq", "dp")),
        P(("seq", "dp")),
        P(("seq", "dp")),
        P(("seq", "dp")),
        P(("seq", "dp")),
        P(("seq", "dp")),
        P(("seq", "dp")),
        P(("seq", "dp"), None),
        P(("seq", "dp"), None),
        P(("seq", "dp"), None),
        P(("seq", "dp"), None),
        P(("seq", "dp")),
        P(("seq", "dp")),
        P(("seq", "dp")),
        P(("seq", "dp")),
        P(("seq", "dp"), None),
        P(("seq", "dp"), None),
        P(("seq", "dp"), None),
    )
    return jax.shard_map(
        per_device,
        mesh=mesh,
        in_specs=placed,
        out_specs=(
            P("dp", "seq", None),
            P("dp", "seq", None),
            P(("seq", "dp")),
            P(("seq", "dp")),
            P(("seq", "dp")),
            P(("seq", "dp")),
            P(("seq", "dp")),
            P(("seq", "dp")),
            P(("seq", "dp")),
            P(("seq", "dp"), None),
            P(("seq", "dp"), None),
            P(("seq", "dp"), None),
            P(("seq", "dp"), None),
            P(("seq", "dp")),
            P(("seq", "dp")),
            P(("seq", "dp")),
            P(("seq", "dp")),
            P(("seq", "dp"), None),
            P(("seq", "dp"), None),
            P(("seq", "dp"), None),
        ),
        check_vma=False,
    )
```

profile of v0, /device:TPU:0, one launch (start us, length us, event | category | flops | bytes accessed | tf_op | source)
XLA Modules:
  0.0 1945.1 jit_solution(14644124119905562639)
XLA Ops:
  20.4 42.5 %all-reduce.23 = (bf16[1024]{0:T(1024)(128)(2,1)S(1)}, bf16[1024]{0:T(1024)(128)(2,1)S(1)}, bf16[1024]{0:T(1024)(128)(2,1)S(1)}, bf16[1024]{0:T(1024)(128)(2,1)S...) all-reduce(bf16[1024]{0:T(1024)(128)(2,1)S(1)} %dynamic-update-slic, ...), channel_id=1, replica_groups=mesh['seq'=4,'dp'=8] {'seq','dp'}, use_global_device_ids=true, to_apply=%add.2 | all-reduce | flops 11264 | bytes 45056
  65.3 1.8 collective-permute-start
  69.1 6.3 all-gather
  75.6 3.5 add_convert_fusion.2
  79.2 3.2 fusion.99
  82.4 46.8 %all-gather.19.cloned.1.call-done = bf16[1024,1024]{1,0:T(8,128)(2,1)} async-done(((bf16[32,1024]{1,0:T(8,128)(2,1)}), bf16[1024,1024]{1,0:T(8,128)(2,1)}) %all-gather.19.cloned.1.call-update) | async-done | bytes 2097168 | tf_op jit(solution)/shard_map/all_gather | solution.py:175
  129.2 4.9 fusion.115
  134.1 5.2 all-gather.5
  139.3 5.4 all-gather.6
  144.9 1.9 copy.103
  150.3 16.6 while.93
  166.8 3.2 copy.65
  170.0 17.6 all-gather.17.cloned.1.call-done
  187.6 5.8 fusion.93
  193.4 52.5 %all-gather.23.cloned.1.call-done = bf16[1024,1024]{1,0:T(8,128)(2,1)} async-done(((bf16[32,1024]{1,0:T(8,128)(2,1)}), bf16[1024,1024]{1,0:T(8,128)(2,1)}) %all-gather.23.cloned.1.call-update) | async-done | bytes 2097168 | tf_op jit(solution)/shard_map/all_gather | solution.py:178
  245.9 3.3 fusion.124
  251.8 2.2 collective-permute-start.1
  254.8 4.6 add_convert_fusion
  259.4 65.6 %all-gather.27.cloned.1.call-done = bf16[1024,4096]{1,0:T(8,128)(2,1)} async-done(((bf16[32,4096]{1,0:T(8,128)(2,1)}), bf16[1024,4096]{1,0:T(8,128)(2,1)}) %all-gather.27.cloned.1.call-update) | async-done | bytes 8388624 | tf_op jit(solution)/shard_map/all_gather | solution.py:183
  325.0 10.5 fusion.66
  335.5 68.4 %all-gather.29.cloned.1.call-done = bf16[4096,1024]{1,0:T(8,128)(2,1)} async-done(((bf16[128,1024]{1,0:T(8,128)(2,1)}), bf16[4096,1024]{1,0:T(8,128)(2,1)}) %all-gather.29.cloned.1.call-update) | async-done | bytes 8388624 | tf_op jit(solution)/shard_map/all_gather | solution.py:185
  403.9 11.7 fusion.62
  415.6 46.5 %all-gather.25.cloned.1.call-done = bf16[1024,1024]{1,0:T(8,128)(2,1)} async-done(((bf16[32,1024]{1,0:T(8,128)(2,1)}), bf16[1024,1024]{1,0:T(8,128)(2,1)}) %all-gather.25.cloned.1.call-update) | async-done | bytes 2097168 | tf_op jit(solution)/shard_map/all_gather | solution.py:184
  462.1 6.5 multiply_convert_fusion.2
  469.6 9.5 multiply_convert_fusion
  479.2 8.7 fusion.64
  487.9 3.6 multiply_reduce_fusion.11
  494.2 3.2 convolution_bitcast_fusion.6
  497.4 3.3 slice.36
  500.8 5.7 multiply_reduce_fusion.13
  510.2 2.5 fusion.96
  517.4 74.4 %while.94 = (s32[]{:T(128)}, f32[64,1024]{1,0:T(8,128)}, f32[64,1024]{1,0:T(8,128)}, f32[64,1024]{1,0:T(8,128)}, f32[1024]{0:T(1024)}, /*index=5*/f32[1024]{0:T(...) while((s32[]{:T(128)}, f32[64,1024]{1,0:T(8,128)}, ...), condition=%wide.region_29.30_spmd.clone.clone.clone, body=%wide.region_14.29_spmd.clone.clone.clone.sunk | while | flops 410291200 | bytes 27583564 | solution.py:108
  519.8 2.1 dynamic-slice_bitcast_fusion.10
  522.7 3.1 multiply_reduce_fusion.29
  536.5 2.1 dynamic-slice_bitcast_fusion.10
  540.0 3.1 multiply_reduce_fusion.29
  545.5 1.7 select_add_fusion.13
  555.7 2.1 dynamic-slice_bitcast_fusion.10
  559.3 3.1 multiply_reduce_fusion.29
  564.7 1.7 select_add_fusion.13
  575.0 2.1 dynamic-slice_bitcast_fusion.10
  578.5 3.1 multiply_reduce_fusion.29
  584.0 1.7 select_add_fusion.13
  585.7 1.7 select_add_fusion.14
  591.9 3.4 copy.69
  596.7 6.2 all-gather.7
  602.9 5.9 all-gather.8
  609.0 6.3 fusion.122
  616.3 3.2 convolution_bitcast_fusion.10
  621.1 3.4 convolution_bitcast_fusion.9
  626.0 3.3 convolution_bitcast_fusion.8
  630.9 4.5 convolution_bitcast_fusion.7
  635.4 12.8 convolution_bitcast_fusion.5
  648.5 14.0 convolution_bitcast_fusion.4
  662.6 3.3 fusion.101
  674.1 3.9 fusion.81
  678.1 44.3 %all-reduce.22 = (f32[1024]{0:T(1024)S(1)}, f32[1024]{0:T(1024)S(1)}, f32[1024]{0:T(1024)S(1)}, f32[1024]{0:T(1024)S(1)}, f32[1024]{0:T(1024)S(1)}, /*index=5*/f...) all-reduce(f32[1024]{0:T(1024)S(1)} %get-tuple-element.1353, ...), channel_id=8, replica_groups=mesh['seq'=4,'dp'=8] {'seq','dp'}, use_global_device_ids=true, to_apply=%region_35.36.clone | all-reduce | flops 11264 | bytes 90112
  728.8 3.6 fusion.80
  732.5 56.5 %reduce-scatter.8.cloned.1.call-done = f32[32,1024]{1,0:T(8,128)} async-done(((f32[1024,1024]{1,0:T(8,128)}), f32[32,1024]{1,0:T(8,128)}) %reduce-scatter.8.cloned.1.call-update) | async-done | bytes 131088 | tf_op jit(solution)/shard_map/reduce_scatter | solution.py:384
  789.0 143.9 %reduce-scatter.10.cloned.1.call-done = f32[32,1024]{1,0:T(8,128)} async-done(((f32[1024,1024]{1,0:T(8,128)}), f32[32,1024]{1,0:T(8,128)}) %reduce-scatter.10.cloned.1.call-update) | async-done | bytes 131088 | tf_op jit(solution)/shard_map/reduce_scatter | solution.py:385
  932.8 142.9 %reduce-scatter.12.cloned.1.call-done = f32[32,1024]{1,0:T(8,128)} async-done(((f32[1024,1024]{1,0:T(8,128)}), f32[32,1024]{1,0:T(8,128)}) %reduce-scatter.12.cloned.1.call-update) | async-done | bytes 131088 | tf_op jit(solution)/shard_map/reduce_scatter | solution.py:386
  1075.7 144.1 %reduce-scatter.14.cloned.1.call-done = f32[32,1024]{1,0:T(8,128)} async-done(((f32[1024,1024]{1,0:T(8,128)}), f32[32,1024]{1,0:T(8,128)}) %reduce-scatter.14.cloned.1.call-update) | async-done | bytes 131088 | tf_op jit(solution)/shard_map/reduce_scatter | solution.py:387
  1219.8 358.2 %reduce-scatter.16.cloned.1.call-done = f32[32,4096]{1,0:T(8,128)} async-done(((f32[1024,4096]{1,0:T(8,128)}), f32[32,4096]{1,0:T(8,128)}) %reduce-scatter.16.cloned.1.call-update) | async-done | bytes 524304 | tf_op jit(solution)/shard_map/reduce_scatter | solution.py:309
  1578.0 360.1 %reduce-scatter.20.cloned.1.call-done = f32[128,1024]{1,0:T(8,128)} async-done(((f32[4096,1024]{1,0:T(8,128)}), f32[128,1024]{1,0:T(8,128)}) %reduce-scatter.20.cloned.1.call-update) | async-done | bytes 524304 | tf_op jit(solution)/shard_map/reduce_scatter | solution.py:299
  (499 shorter events, 120.8 us)
Async XLA Ops:
  7.2 57.2 %copy-start.4 = (bf16[2,256,1024]{2,1,0:T(8,128)(2,1)S(1)}, bf16[2,256,1024]{2,1,0:T(8,128)(2,1)}, u32[]{:S(2)}) copy-start(bf16[2,256,1024]{2,1,0:T(8,128)(2,1)} %param.29) | copy-start | bytes 3145732
  7.2 72.0 %all-gather.21.cloned.1.call-start = ((), (), s32[]{:S(2)}) async-start(), calls=%async_computation.9 | async-start | bytes 2162688 | tf_op jit(solution)/shard_map/all_gather | solution.py:176
  7.9 121.3 %all-gather.19.cloned.1.call-start = ((), (), s32[]{:S(2)}) async-start(), calls=%async_computation.8 | async-start | bytes 2162688 | tf_op jit(solution)/shard_map/all_gather | solution.py:175
  8.7 178.9 %all-gather.17.cloned.1.call-start = ((), (), s32[]{:S(2)}) async-start(), calls=%async_computation.7 | async-start | bytes 2162688 | tf_op jit(solution)/shard_map/all_gather | solution.py:177
  9.4 236.4 %all-gather.23.cloned.1.call-start = ((), (), s32[]{:S(2)}) async-start(), calls=%async_computation.10 | async-start | bytes 2162688 | tf_op jit(solution)/shard_map/all_gather | solution.py:178
  10.0 315.0 %all-gather.27.cloned.1.call-start = ((), (), s32[]{:S(2)}) async-start(), calls=%async_computation.12 | async-start | bytes 8650752 | tf_op jit(solution)/shard_map/all_gather | solution.py:183
  10.6 393.3 %all-gather.29.cloned.1.call-start = ((), (), s32[]{:S(2)}) async-start(), calls=%async_computation.13 | async-start | bytes 8650752 | tf_op jit(solution)/shard_map/all_gather | solution.py:185
  11.2 450.9 %all-gather.25.cloned.1.call-start = ((), (), s32[]{:S(2)}) async-start(), calls=%async_computation.11 | async-start | bytes 2162688 | tf_op jit(solution)/shard_map/all_gather | solution.py:184
  62.9 4.9 copy-start.82
  62.9 12.6 copy-start.62
  63.0 12.6 copy-start.56
  64.4 11.1 copy-start.60
  64.9 10.7 copy-start.64
  65.3 13.8 copy-start.8
  65.3 10.1 collective-permute-start
  67.2 665.2 %reduce-scatter.18.cloned.1.call-start = ((), (), s32[]{:S(2)}) async-start(), calls=%async_computation.19 | async-start | bytes 4325376 | tf_op jit(solution)/shard_map/reduce_scatter | solution.py:303
  67.3 8.2 copy-start.84
  67.8 11.3 copy-start.76
  69.0 10.1 copy-start.66
  69.0 10.1 copy-start.68
  69.0 10.1 copy-start.70
  69.1 10.1 copy-start.72
  69.1 10.1 copy-start.74
  82.4 51.7 %copy-start.12 = (f32[2,256,1024]{2,1,0:T(8,128)}, f32[2,256,1024]{2,1,0:T(8,128)S(1)}, u32[]{:S(2)}) copy-start(f32[2,256,1024]{2,1,0:T(8,128)S(1)} %fusion.99) | copy-start | bytes 6291460
  249.5 4.5 copy-start.86
  251.8 3.0 collective-permute-start.1
  259.4 76.1 %copy-start.27 = (bf16[2,256,1024]{2,1,0:T(8,128)(2,1)}, bf16[2,256,1024]{2,1,0:T(8,128)(2,1)S(1)}, u32[]{:S(2)}) copy-start(bf16[2,256,1024]{2,1,0:T(8,128)(2,1)S(1)} %get-tuple-element.1523) | copy-start | bytes 3145732
  403.9 58.1 %copy-start.36 = (bf16[2,256,1024]{2,1,0:T(8,128)(2,1)S(1)}, bf16[2,256,1024]{2,1,0:T(8,128)(2,1)}, u32[]{:S(2)}) copy-start(bf16[2,256,1024]{2,1,0:T(8,128)(2,1)} %param.31) | copy-start | bytes 3145732
  479.1 8.7 copy-start.25
  479.1 8.7 copy-start.7
  479.2 8.7 copy-start.30
  479.2 8.7 copy-start.40
  487.9 3.7 copy-start.20
  487.9 6.3 copy-start.39
  492.8 7.9 collective-permute-start.2
  500.7 288.2 %reduce-scatter.8.cloned.1.call-start = ((), (), s32[]{:S(2)}) async-start(), calls=%async_computation.14 | async-start | bytes 4325376 | tf_op jit(solution)/shard_map/reduce_scatter | solution.py:384
  500.8 5.7 copy-start.3
  506.5 3.7 copy-start.31
  507.4 5.3 copy-start.10
  529.6 3.9 copy-start.50
  529.6 3.9 copy-start.53
  548.9 3.9 copy-start.50
  548.9 3.9 copy-start.53
  568.1 3.9 copy-start.50
  568.1 3.9 copy-start.53
  587.4 3.9 copy-start.50
  587.4 3.9 copy-start.53
  595.3 13.7 copy-start.14
  595.3 13.7 copy-start.15
  609.0 7.3 copy-start.24
  619.5 313.3 %reduce-scatter.10.cloned.1.call-start = ((), (), s32[]{:S(2)}) async-start(), calls=%async_computation.15 | async-start | bytes 4325376 | tf_op jit(solution)/shard_map/reduce_scatter | solution.py:385
  624.5 451.3 %reduce-scatter.12.cloned.1.call-start = ((), (), s32[]{:S(2)}) async-start(), calls=%async_computation.16 | async-start | bytes 4325376 | tf_op jit(solution)/shard_map/reduce_scatter | solution.py:386
  629.3 590.5 %reduce-scatter.14.cloned.1.call-start = ((), (), s32[]{:S(2)}) async-start(), calls=%async_computation.17 | async-start | bytes 4325376 | tf_op jit(solution)/shard_map/reduce_scatter | solution.py:387
  635.3 942.6 %reduce-scatter.16.cloned.1.call-start = ((), (), s32[]{:S(2)}) async-start(), calls=%async_computation.18 | async-start | bytes 17301504 | tf_op jit(solution)/shard_map/reduce_scatter | solution.py:309
  648.2 1289.8 %reduce-scatter.20.cloned.1.call-start = ((), (), s32[]{:S(2)}) async-start(), calls=%async_computation.20 | async-start | bytes 17301504 | tf_op jit(solution)/shard_map/reduce_scatter | solution.py:299
  667.7 4.4 copy-start.52
  667.7 4.4 copy-start.55
  667.7 4.4 copy-start.83
  669.2 3.4 collective-permute-start.3
  674.1 4.0 copy-start.49
  674.1 4.0 copy-start.78
  674.1 3.9 copy-start.79
  674.1 3.9 copy-start.80
  674.1 3.9 copy-start.81
  (78 other events, 151.4 us)
Sparse Core Ops, SparseCore 0:
  11.0 59.6 all-gather.20
  73.7 55.5 all-gather.18
  132.2 55.3 all-gather.16
  190.4 55.3 all-gather.22
  248.7 76.3 all-gather.26
  327.9 75.9 all-gather.28
  406.9 55.1 all-gather.24
  500.8 144.2 reduce-scatter.17
  648.0 140.9 reduce-scatter.7
  791.7 141.1 reduce-scatter.9
  935.7 139.9 reduce-scatter.11
  1078.4 141.3 reduce-scatter.13
  1222.7 355.2 reduce-scatter.15
  1580.7 357.3 reduce-scatter.19
where the time goes:
time: 1950 us
  waiting for transfers between devices  1510 us (77%)
  matrix products  152 us (8%)
  blocking collectives  116 us (6%)
  other arithmetic  75.3 us (4%)
  local copies, waits for them, and re-layouts  70.8 us (4%)
    reduce_scatter x1, waiting for transfers between devices, per_device(): lax.psum_scatter(matmul('nlf,nld->fd', rows_in, down_grad), ('seq', 'dp')...  360 us
    reduce_scatter x1, waiting for transfers between devices, per_device(): lax.psum_scatter(matmul('nlc,nlf->cf', rows_in, up_grad), ('seq', 'dp'),...  358 us
    reduce_scatter x1, waiting for transfers between devices, per_device(): lax.psum_scatter(grad_output, ('seq', 'dp'), scatter_dimension=0, tiled=T...  144 us
    reduce_scatter x1, waiting for transfers between devices, per_device(): lax.psum_scatter(grad_value, ('seq', 'dp'), scatter_dimension=0, tiled=True)  144 us
    reduce_scatter x1, waiting for transfers between devices, per_device(): lax.psum_scatter(grad_recept, ('seq', 'dp'), scatter_dimension=0, tiled=T...  143 us
    dot_general x21, matrix products, matmul(): return jnp.einsum(form, left, right, preferred_element_type=jnp.float32)  121 us
    unnamed x2, blocking collectives  86.8 us
    all_gather x1, waiting for transfers between devices, per_device(): lax.all_gather(shards[17], ('seq', 'dp'), axis=0, tiled=True)  68.4 us
  transfers between devices with their start and end apart: 18, of which 13 were waited for; matrix products, arithmetic and copies ran while one was open for 13% of the time, Pallas kernels for 0%

commit v1 on v0

v1 whole, which is shorter than its diff:
```python
import jax
import jax.numpy as jnp
from jax import lax
from jax.sharding import PartitionSpec as P

BLK = 64


EPS = 1e-05

def norm_stats(field):
    center = field - jnp.mean(field, axis=-1, keepdims=True)
    inverse = lax.rsqrt(jnp.mean(center * center, axis=-1, keepdims=True) + EPS)
    return (center * inverse, inverse)


def norm_back(grad_normed, normalized, inverse):
    mean_grad = jnp.mean(grad_normed, axis=-1, keepdims=True)
    mean_proj = jnp.mean(grad_normed * normalized, axis=-1, keepdims=True)
    return inverse * (grad_normed - mean_grad - normalized * mean_proj)


def summary(lookup_matrix_output, content_matrix_output, fading_rate_vector):
    span_len = lookup_matrix_output.shape[1]
    distance = (span_len - 1 - jnp.arange(span_len, dtype=jnp.float32))[:, None]
    weight = jnp.exp(lookup_matrix_output - distance * fading_rate_vector)
    return (jnp.sum(weight * content_matrix_output, axis=1), jnp.sum(weight, axis=1))


def combine_state(earlier, later):
    return (
        earlier[0] * later[0],
        later[0] * earlier[1] + later[1],
        later[0] * earlier[2] + later[2],
    )


def compute_attention_recurrence(
    lookup_matrix_output,
    content_matrix_output,
    fading_rate_vector,
    boost_log_scale,
    starting_accumulator,
    starting_normalizer,
):
    seq_count, span_len, channels = lookup_matrix_output.shape
    blocks = span_len // BLK
    offset = jnp.arange(BLK, dtype=jnp.float32)[:, None]
    strict_lower = (jnp.arange(BLK)[:, None] > jnp.arange(BLK)[None, :]).astype(jnp.float32)
    rising = jnp.exp(offset * fading_rate_vector)
    falling = jnp.exp(-offset * fading_rate_vector)
    carry_fall = jnp.exp((1.0 - offset) * fading_rate_vector)
    end_fall = jnp.exp(-BLK * fading_rate_vector)
    end_carry = jnp.exp((1.0 - BLK) * fading_rate_vector)

    def one_block(state, inputs):
        state_a, state_b = state
        lookup_piece_entries, content_piece_entries = inputs
        weight = jnp.exp(lookup_piece_entries) * rising
        weighted = weight * content_piece_entries
        sum_a = jnp.einsum("ts,nsc->ntc", strict_lower, weighted, precision=lax.Precision.HIGHEST)
        sum_b = jnp.einsum("ts,nsc->ntc", strict_lower, weight, precision=lax.Precision.HIGHEST)
        earlier_accumulator = falling * state_a[:, None, :] + carry_fall * sum_a
        earlier_normalizer = falling * state_b[:, None, :] + carry_fall * sum_b
        current_token_boost = jnp.exp(boost_log_scale + lookup_piece_entries)
        module_output_tensor = (
            earlier_accumulator + current_token_boost * content_piece_entries
        ) / (earlier_normalizer + current_token_boost)
        next_a = end_fall * state_a + end_carry * jnp.sum(weighted, axis=1)
        next_b = end_fall * state_b + end_carry * jnp.sum(weight, axis=1)
        return ((next_a, next_b), module_output_tensor)

    key_seq = jnp.moveaxis(lookup_matrix_output.reshape(seq_count, blocks, BLK, channels), 1, 0)
    value_seq = jnp.moveaxis(content_matrix_output.reshape(seq_count, blocks, BLK, channels), 1, 0)
    final_state, results = lax.scan(
        jax.checkpoint(one_block), (starting_accumulator, starting_normalizer), (key_seq, value_seq)
    )
    return jnp.moveaxis(results, 0, 1).reshape(seq_count, span_len, channels)


SEQ = ("y", "core")
DP = ("z", "x")
ALL = ("y", "core", "z", "x")


def matmul(form, left, right):
    return jnp.einsum(form, left, right, preferred_element_type=jnp.float32)


def shifted(block, axis, distance):
    count = lax.axis_size(axis)
    route = [(i - distance, i) for i in range(count) if 0 <= i - distance < count]
    return lax.ppermute(block, axis, route)


def previous_rows(field):
    came = shifted(field[:, -1, :], SEQ, 1)
    return jnp.concatenate([came[:, None, :], field[:, :-1, :]], axis=1)


def next_rows(field):
    came = shifted(field[:, 0, :], SEQ, -1)
    return jnp.concatenate([field[:, 1:, :], came[:, None, :]], axis=1)


def prefix(x, reverse):
    count, mine = (lax.axis_size(SEQ), lax.axis_index(SEQ))
    factor, a, b = x
    every = lax.all_gather(jnp.stack([a, b]), SEQ)
    total = jnp.zeros_like(every[0])
    for k in range(count):
        at = count - 1 - k if reverse else k
        reached = at > mine if reverse else at < mine
        total = jnp.where(reached, factor * total + every[at], total)
    return (total[0], total[1])


def rs_axis(parts, dim, axis, kind):
    count, mine = (lax.axis_size(axis), lax.axis_index(axis))

    def take(j):
        taken = [lax.dynamic_index_in_dim(p, j, dim, keepdims=False) for p in parts]
        return taken[0] if len(taken) == 1 else jnp.concatenate(taken, axis=-2)

    came = []
    for k in range(1, count):
        route = [(i, (i + k) % count) for i in range(count)]
        block = take(lax.rem(mine + k, count)).astype(jnp.bfloat16)
        came.append(lax.ppermute(block, axis, route))
    total = take(mine).astype(jnp.float32)
    for block in came:
        total = total + block.astype(jnp.float32)
    return total.astype(kind)


def reduce_scatter(parts):
    low = jnp.bfloat16
    g = rs_axis(parts, 1, "core", low)
    half = g.shape[-1] // 2
    a, b = (g[..., :half], g[..., half:])
    a = rs_axis([a], 2, "x", low)
    b = rs_axis([b], 0, "y", low)
    a = rs_axis([a], 0, "y", low)
    b = rs_axis([b], 1, "x", low)
    return rs_axis([jnp.concatenate([a, b], axis=-1)], 0, "z", jnp.float32)


def per_device(
    tokens,
    lengths,
    cotangent,
    first_gain,
    first_bias,
    mix_key,
    mix_value,
    mix_recept,
    time_decay,
    time_first,
    key_weight,
    value_weight,
    recept_weight,
    output_weight,
    second_gain,
    second_bias,
    shift_key,
    shift_recept,
    up_weight,
    gate_weight,
    down_weight,
):
    grid = tuple(lax.axis_size(axis) for axis in ALL)
    count = grid[0] * grid[1] * grid[2] * grid[3]
    seq_count, piece_len, channels = tokens.shape
    hidden = up_weight.shape[1]
    mine = channels // count
    blocks = hidden // channels

    vectors = (
        first_gain,
        first_bias,
        mix_key,
        mix_value,
        mix_recept,
        time_decay,
        time_first,
        second_gain,
        second_bias,
        shift_key,
        shift_recept,
    )
    n_vec = len(vectors)
    flat = jnp.concatenate(vectors)
    packed = jnp.pad(flat, (0, 8 * channels - n_vec * mine)).reshape(8, channels)
    early = lax.all_gather(
        jnp.concatenate([key_weight, value_weight, recept_weight, packed]), ALL, axis=0
    )
    late = lax.all_gather(
        jnp.concatenate(
            [output_weight]
            + [up_weight[:, j * channels : (j + 1) * channels] for j in range(blocks)]
            + [gate_weight, down_weight]
        ),
        ALL,
        axis=0,
    )

    def square(gathered, at, rows=mine):
        return gathered[:, at : at + rows].reshape(count * rows, channels)

    key_mat, value_mat, recept_mat = (square(early, j * mine) for j in range(3))
    vecs = early[:, 3 * mine].reshape(count, -1)[:, : n_vec * mine].reshape(count, n_vec, mine)
    vecs = jnp.moveaxis(vecs, 1, 0).reshape(n_vec, channels).astype(jnp.float32)
    (
        norm_gain,
        norm_bias,
        key_mix,
        value_mix,
        recept_mix,
        decay_log,
        boost_log_scale,
        gain_two,
        bias_two,
        chan_key_mix,
        chan_recept_mix,
    ) = (vecs[j] for j in range(n_vec))
    output_mat = square(late, 0)
    up_mat = jnp.concatenate([square(late, (1 + j) * mine) for j in range(blocks)], axis=1)
    gate_mat = square(late, (1 + blocks) * mine)
    down_mat = square(late, (2 + blocks) * mine, hidden // count)

    seq_index = lax.axis_index(SEQ)
    positions = seq_index * piece_len + jnp.arange(piece_len, dtype=jnp.int32)
    live_mask = (positions[None, :] < lengths[:, None]).astype(jnp.float32)[:, :, None]
    field = tokens.astype(jnp.float32)
    normed_one, inverse_one = norm_stats(field)
    normed = normed_one * norm_gain + norm_bias
    before = previous_rows(normed)
    key_in = (normed * key_mix + before * (1.0 - key_mix)).astype(jnp.bfloat16)
    value_in = (normed * value_mix + before * (1.0 - value_mix)).astype(jnp.bfloat16)
    recept_in = (normed * recept_mix + before * (1.0 - recept_mix)).astype(jnp.bfloat16)
    lookup_matrix_output = matmul("nlc,cd->nld", key_in, key_mat)
    content_matrix_output = matmul("nlc,cd->nld", value_in, value_mat)
    recept_proj = matmul("nlc,cd->nld", recept_in, recept_mat)
    fading_rate_vector = jnp.exp(decay_log)
    (local_a, local_b), summary_pull = jax.vjp(
        summary, lookup_matrix_output, content_matrix_output, fading_rate_vector
    )
    piece_fall = jnp.exp(-piece_len * fading_rate_vector)
    starting_accumulator, starting_normalizer = prefix((piece_fall, local_a, local_b), False)
    blended, weighted_kv_pullback = jax.vjp(
        compute_attention_recurrence,
        lookup_matrix_output,
        content_matrix_output,
        fading_rate_vector,
        boost_log_scale,
        starting_accumulator,
        starting_normalizer,
    )
    recept_sig = jax.nn.sigmoid(recept_proj)
    mixed_out = (recept_sig * blended).astype(jnp.bfloat16)
    branch = matmul("nlc,cd->nld", mixed_out, output_mat)
    residual = field + branch
    normed_two_raw, inverse_two = norm_stats(residual)
    normed_two = normed_two_raw * gain_two + bias_two
    before_two = previous_rows(normed_two)
    ffn_key = (normed_two * chan_key_mix + before_two * (1.0 - chan_key_mix)).astype(jnp.bfloat16)
    ffn_recept = (normed_two * chan_recept_mix + before_two * (1.0 - chan_recept_mix)).astype(
        jnp.bfloat16
    )
    up_proj = matmul("nlc,cf->nlf", ffn_key, up_mat)
    squared = jnp.square(jax.nn.relu(up_proj)).astype(jnp.bfloat16)
    down_proj = matmul("nlf,fd->nld", squared, down_mat)
    gate_value = jax.nn.sigmoid(matmul("nlc,cd->nld", ffn_recept, gate_mat))
    output = ((residual + gate_value * down_proj) * live_mask).astype(jnp.bfloat16)

    def outer(left, right):
        whole = jnp.einsum("nlc,nld->cd", left, right, preferred_element_type=jnp.float32)
        return whole.astype(jnp.bfloat16).reshape(*grid, -1, right.shape[-1])

    def by_columns(g):
        return [g[..., j * channels : (j + 1) * channels] for j in range(g.shape[-1] // channels)]

    seed = cotangent.astype(jnp.float32) * live_mask
    down_grad = (seed * gate_value).astype(jnp.bfloat16)
    gate_grad = (seed * down_proj * gate_value * (1.0 - gate_value)).astype(jnp.bfloat16)
    first = reduce_scatter([outer(squared, down_grad), outer(ffn_recept, gate_grad)])
    squared_grad = matmul("nld,fd->nlf", down_grad, down_mat)
    up_grad = (squared_grad * 2.0 * jax.nn.relu(up_proj)).astype(jnp.bfloat16)
    grad_up_part = by_columns(outer(ffn_key, up_grad))
    ffn_key_grad = matmul("nlf,cf->nlc", up_grad, up_mat)
    ffn_recept_grad = matmul("nld,cd->nlc", gate_grad, gate_mat)
    normed_two_grad = (
        ffn_key_grad * chan_key_mix
        + ffn_recept_grad * chan_recept_mix
        + next_rows(ffn_key_grad * (1.0 - chan_key_mix) + ffn_recept_grad * (1.0 - chan_recept_mix))
    )
    gap_two = normed_two - before_two
    grad_chan_key = jnp.sum(ffn_key_grad * gap_two, axis=(0, 1))
    grad_chan_recept = jnp.sum(ffn_recept_grad * gap_two, axis=(0, 1))
    grad_gain_two = jnp.sum(normed_two_grad * normed_two_raw, axis=(0, 1))
    grad_bias_two = jnp.sum(normed_two_grad, axis=(0, 1))
    residual_grad = seed + norm_back(normed_two_grad * gain_two, normed_two_raw, inverse_two)
    branch_grad = residual_grad.astype(jnp.bfloat16)
    second = reduce_scatter(grad_up_part + [outer(mixed_out, branch_grad)])
    mixed_grad = matmul("nld,cd->nlc", branch_grad, output_mat)
    recept_grad = (mixed_grad * blended * recept_sig * (1.0 - recept_sig)).astype(jnp.bfloat16)
    blended_grad = mixed_grad * recept_sig
    (
        key_gradient_first,
        value_gradient_first,
        decay_gradient_first,
        boost_adjoint_term,
        initial_numerator_gradient,
        initial_denominator_gradient,
    ) = weighted_kv_pullback(blended_grad)
    carry_a, carry_b = prefix(
        (piece_fall, initial_numerator_gradient, initial_denominator_gradient), True
    )
    key_grad_b, value_grad_b, rate_grad_b = summary_pull((carry_a, carry_b))
    factor_grad = jnp.sum(carry_a * starting_accumulator + carry_b * starting_normalizer, axis=0)
    rate_grad = decay_gradient_first + rate_grad_b - piece_len * piece_fall * factor_grad
    grad_decay = rate_grad * fading_rate_vector
    key_grad = (key_gradient_first + key_grad_b).astype(jnp.bfloat16)
    value_grad = (value_gradient_first + value_grad_b).astype(jnp.bfloat16)
    key_in_grad = matmul("nld,cd->nlc", key_grad, key_mat)
    value_in_grad = matmul("nld,cd->nlc", value_grad, value_mat)
    recept_in_grad = matmul("nld,cd->nlc", recept_grad, recept_mat)
    normed_grad = (
        key_in_grad * key_mix
        + value_in_grad * value_mix
        + recept_in_grad * recept_mix
        + next_rows(
            key_in_grad * (1.0 - key_mix)
            + value_in_grad * (1.0 - value_mix)
            + recept_in_grad * (1.0 - recept_mix)
        )
    )
    gap_one = normed - before
    grad_key_mix = jnp.sum(key_in_grad * gap_one, axis=(0, 1))
    grad_value_mix = jnp.sum(value_in_grad * gap_one, axis=(0, 1))
    grad_recept_mix = jnp.sum(recept_in_grad * gap_one, axis=(0, 1))
    grad_gain_one = jnp.sum(normed_grad * normed_one, axis=(0, 1))
    grad_bias_one = jnp.sum(normed_grad, axis=(0, 1))
    tokens_grad = residual_grad + norm_back(normed_grad * norm_gain, normed_one, inverse_one)
    sums = jnp.stack(
        [
            grad_gain_one,
            grad_bias_one,
            grad_key_mix,
            grad_value_mix,
            grad_recept_mix,
            grad_decay,
            boost_adjoint_term,
            grad_gain_two,
            grad_bias_two,
            grad_chan_key,
            grad_chan_recept,
        ]
    )
    sums = jnp.moveaxis(sums.reshape(n_vec, *grid, mine), 0, -2).reshape(*grid, n_vec * mine)
    padding = [(0, 0)] * 4 + [(0, 8 * channels - n_vec * mine)]
    sums = jnp.pad(sums, padding).reshape(*grid, 8, channels).astype(jnp.bfloat16)
    third = reduce_scatter(
        [outer(key_in, key_grad), outer(value_in, value_grad), outer(recept_in, recept_grad), sums]
    )
    vec_out = third[3 * mine :].reshape(-1)[: n_vec * mine].reshape(n_vec, mine)
    rows_down = hidden // count
    return (
        output,
        tokens_grad,
        *(vec_out[j] for j in range(7)),
        *(third[j * mine : (j + 1) * mine] for j in range(3)),
        second[blocks * mine :],
        *(vec_out[j] for j in range(7, n_vec)),
        jnp.concatenate([second[j * mine : (j + 1) * mine] for j in range(blocks)], axis=1),
        first[rows_down:],
        first[:rows_down],
    )


def solution(mesh):
    seq, dp = (mesh.shape["seq"], mesh.shape["dp"])
    wide = len({device.coords[0] for device in mesh.devices.reshape(-1)})
    fine = jax.sharding.Mesh(mesh.devices.reshape(seq // 2, 2, dp // wide, wide), ALL)
    field, vector, matrix = (P(DP, SEQ, None), P(ALL), P(ALL, None))
    return jax.shard_map(
        per_device,
        mesh=fine,
        in_specs=(field, P(DP), field) + (vector,) * 7 + (matrix,) * 4 + (vector,) * 4 + (matrix,) * 3,
        out_specs=(field, field) + (vector,) * 7 + (matrix,) * 4 + (vector,) * 4 + (matrix,) * 3,
        check_vma=False,
    )
```

time: 1950 us -> 719 us (0.37)
  waiting for transfers between devices: 1510 us -> 280 us
  blocking collectives: 116 us -> 13.1 us
  local copies, waits for them, and re-layouts: 70.8 us -> 148 us
  starting transfers between devices: 7.38 us -> 47.6 us
  matrix products: 152 us -> 114 us
    reduce_scatter x7 -> x0, waiting for transfers between devices: 1210 us -> none  [the longest x1 360 us: per_device(): lax.psum_scatter(matmul('nlf,nld->fd', rows_in, down_grad), ('seq', 'dp')...]
    all_gather x7 -> x2, waiting for transfers between devices: 297 us -> 149 us  [the longest x1 82.7 us: per_device(): lax.all_gather(jnp.concatenate([output_weight] + [up_weight[:, j * channe...]
    ppermute x0 -> x24, waiting for transfers between devices: none -> 132 us  [rs_axis(): came.append(lax.ppermute(block, axis, route))]
    unnamed x2 -> x0, blocking collectives: 86.8 us -> none
    dot_general x21 -> x14, matrix products: 121 us -> 62.6 us  [matmul(): return jnp.einsum(form, left, right, preferred_element_type=jnp.float32)]
    ppermute x0 -> x24, starting transfers between devices: none -> 39.9 us  [rs_axis(): came.append(lax.ppermute(block, axis, route))]
    slice x4 -> x17, local copies, waits for them, and re-layouts: 0.03 us -> 34.5 us  [the longest x3 23.5 us: square(): return gathered[:, at:at + rows].reshape(count * rows, channels)]
    dynamic_slice x0 -> x23, local copies, waits for them, and re-layouts: none -> 27.6 us  [take(): taken = [lax.dynamic_index_in_dim(p, j, dim, keepdims=False) for p in parts]]
  transfers between devices with their start and end apart: 18 -> 30, of which waited for: 13 -> 15; matrix products, arithmetic and copies ran while one was open for 13% -> 19% of each run, Pallas kernels for 0% -> 0%
where the time goes in v1:
time: 719 us; the launch traced here: 711 us
  waiting for transfers between devices  280 us (39%)
  local copies, waits for them, and re-layouts  148 us (21%)
  matrix products  114 us (16%)
  other arithmetic  90.3 us (13%)
  starting transfers between devices  47.6 us (7%)
  between operations  16.5 us (2%)
  blocking collectives  13.1 us (2%)
    ppermute x24, waiting for transfers between devices, rs_axis(): came.append(lax.ppermute(block, axis, route))  132 us
    all_gather x1, waiting for transfers between devices, per_device(): lax.all_gather(jnp.concatenate([output_weight] + [up_weight[:, j * channe...  82.7 us
    all_gather x1, waiting for transfers between devices, per_device(): lax.all_gather(jnp.concatenate([key_weight, value_weight, recept_weight,...  66.1 us
    dot_general x14, matrix products, matmul(): return jnp.einsum(form, left, right, preferred_element_type=jnp.float32)  62.6 us
    ppermute x24, starting transfers between devices, rs_axis(): came.append(lax.ppermute(block, axis, route))  39.9 us
    unnamed x259, local copies, waits for them, and re-layouts  34.8 us
    dynamic_slice x23, local copies, waits for them, and re-layouts, take(): taken = [lax.dynamic_index_in_dim(p, j, dim, keepdims=False) for p in parts]  27.6 us
    slice x3, local copies, waits for them, and re-layouts, square(): return gathered[:, at:at + rows].reshape(count * rows, channels)  23.5 us
  transfers between devices with their start and end apart: 30, of which 15 were waited for; matrix products, arithmetic and copies ran while one was open for 19% of the time, Pallas kernels for 0%

profile of v1, /device:TPU:0, one launch (start us, length us, event | category | flops | bytes accessed | tf_op | source)
XLA Modules:
  0.0 710.6 jit_solution(2470953814875141319)
XLA Ops:
  7.3 7.5 %concatenate.56 = bf16[352]{0:T(512)(128)(2,1)S(1)} concatenate(bf16[32]{0:T(256)(128)(2,1)} %param.28, bf16[32]{0:T(256)(128)(2,1)} %param.29, bf16[32]{0:T(256)(128)(2,1)} %param.30, bf16[32]{0:T(256)(128)(2,1)} %param.31, bf16[32]{0:T(256)(128)(2,1)} %param.32, bf16[32]{0:T(256)(128)(2,1)} %param.33, bf16[32]{0:T(256)(128)(2,1)} %param.34, bf16[32]{0:T(256)(128)(2,1)} %param.39, ...), dimensions={0} | concatenate | bytes 1408 | tf_op jit(solution)/shard_map/concatenate | solution.py:192
  24.8 66.1 %all-gather.7.cloned.1.call-done = bf16[3328,1024]{1,0:T(8,128)(2,1)} async-done(((bf16[104,1024]{1,0:T(8,128)(2,1)}), bf16[3328,1024]{1,0:T(8,128)(2,1)}) %all-gather.7.cloned.1.call-update) | async-done | bytes 6815760 | tf_op jit(solution)/shard_map/all_gather | solution.py:194
  93.6 2.2 collective-permute-start
  97.1 5.9 fusion.143
  103.7 2.8 add_convert_fusion.6
  113.8 6.1 all-gather.1
  121.6 16.6 %while.57 = (s32[]{:T(128)}, f32[2,1024]{1,0:T(2,128)S(1)}, f32[2,1024]{1,0:T(2,128)S(1)}, f32[4,2,64,1024]{3,2,1,0:T(8,128)}, f32[4,2,1024]{2,1,0:T(2,128)}, /*...) while((s32[]{:T(128)}, f32[2,1024]{1,0:T(2,128)S(1)}, ...), condition=%wide.region_7.8_spmd.clone.clone.clone, body=%wide.region_4.7_spmd.clone.clone.clone.sunk | while | flops 204038144 | bytes 16915128 | solution.py:75
  141.5 3.3 fusion.77
  144.7 82.7 %all-gather.9.cloned.1.call-done = bf16[10240,1024]{1,0:T(8,128)(2,1)} async-done(((bf16[320,1024]{1,0:T(8,128)(2,1)}), bf16[10240,1024]{1,0:T(8,128)(2,1)}) %all-gather.9.cloned.1.call-update) | async-done | bytes 20971536 | tf_op jit(solution)/shard_map/all_gather | solution.py:197
  227.4 9.2 %fusion.141 = (bf16[32,32,1024]{2,1,0:T(8,128)(2,1)}, bf16[32,32,1024]{2,1,0:T(8,128)(2,1)}, bf16[32,32,1024]{2,1,0:T(8,128)(2,1)}, bf16[32,32,1024]{2,1,0:T(8,1...) fusion(bf16[32,320,1024]{2,1,0:T(8,128)(2,1)} %bitcast.493), kind=kLoop, calls=%fused_computation.424 | loop fusion | bytes 25165824 | tf_op jit(solution)/shard_map/slice | solution.py:208
  241.0 2.7 collective-permute-start.1
  244.4 8.4 %slice.390 = bf16[32,128,1024]{2,1,0:T(8,128)(2,1)} slice(bf16[32,320,1024]{2,1,0:T(8,128)(2,1)} %bitcast.494), slice={[0:32], [192:320], [0:1024]} | slice | bytes 16777216 | tf_op jit(solution)/shard_map/slice | solution.py:208
  252.8 3.1 add_convert_fusion.3
  256.0 10.1 %fusion.57 = f32[2,256,4096]{2,1,0:T(8,128)} fusion(bf16[2,256,1024]{2,1,0:T(8,128)(2,1)S(1)} %get-tuple-element.1147, bf16[1024,1024]{1,0:T(8,128)(2,1)} %bitcast.534, bf16[1024,1024]{1,0:T(8,128)(2,1)} %bitcast.536, bf16[1024,1024]{1,0:T(8,128)(2,1)} %bitcast.538, bf16[1024,1024]{1,0:T(8,128)(2,1)S(1)} %bitcast.532), kind=kOutput, calls=%fused_computation.120 | convolution fusion | flops 4328521728 | bytes 17825792 | tf_op jit(solution)/shard_map/nlc,cf->nlf/dot_general | solution.py:87
  266.1 7.6 %fusion.89 = f32[2,256,1024]{2,1,0:T(8,128)S(1)} fusion(bf16[4096,1024,1]{1,0,2:T(8,128)(2,1)S(1)} %bitcast.509, f32[2,256,4096]{2,1,0:T(8,128)} %fusion.57), kind=kOutput, calls=%fused_computation.234 | convolution fusion | flops 4301258752 | bytes 18874368 | tf_op jit(solution)/shard_map/nlf,fd->nld/dot_general | solution.py:87
  273.7 3.8 multiply_convert_fusion.2
  277.6 12.9 %multiply_convert_fusion = bf16[2,256,4096]{2,1,0:T(8,128)(2,1)} fusion(f32[2,256,4096]{2,1,0:T(8,128)} %fusion.57, bf16[2,256,1024]{2,1,0:T(8,128)(2,1)} %get-tuple-element.1160, bf16[4096,1024,1]{1,0,2:T(8,128)(2,1)} %bitcast.506), kind=kOutput, calls=%fused_computation.108 | convolution fusion | flops 4303355904 | bytes 22020096 | tf_op jit(solution)/shard_map/nld,fd->nlf/dot_general | solution.py:87
  290.5 7.7 %fusion.56 = f32[2,256,1024]{2,1,0:T(8,128)S(1)} fusion(bf16[2,256,4096]{2,1,0:T(8,128)(2,1)} %multiply_convert_fusion, bf16[1024,1024]{1,0:T(8,128)(2,1)S(1)} %bitcast.535, bf16[1024,1024]{1,0:T(8,128)(2,1)S(1)} %bitcast.537, bf16[1024,1024]{1,0:T(8,128)(2,1)} %bitcast.539, bf16[1024,1024]{1,0:T(8,128)(2,1)S(1)} %bitcast.533), kind=kOutput, calls=%fused_computation.119 | convolution fusion | flops 4328521728 | bytes 14680064 | tf_op jit(solution)/shard_map/nlf,cf->nlc/dot_general | solution.py:87
  298.2 7.0 bitcast_convert_fusion.1
  305.2 8.3 %bitcast_convert_fusion = bf16[4096,1024]{1,0:T(8,128)(2,1)S(1)} fusion(bf16[2,256,1024]{2,1,0:T(8,128)(2,1)} %get-tuple-element.1160, f32[2,256,4096]{2,1,0:T(8,128)} %fusion.57), kind=kOutput, calls=%fused_computation.103 | convolution fusion | flops 4305453056 | bytes 17825792 | tf_op jit(solution)/shard_map/nlc,nld->cd/dot_general | solution.py:277
  313.5 2.6 bitcast_convert_fusion.2
  316.2 5.4 multiply_reduce_fusion.11
  322.9 4.1 fusion.142
  327.0 4.6 constant_dynamic-slice_fusion.3
  331.6 2.8 constant_dynamic-slice_fusion.2
  338.4 5.1 copy.258
  344.6 2.3 multiply_reduce_fusion.13
  350.5 2.5 fusion.80
  357.6 65.6 %while.58 = (s32[]{:T(128)}, f32[64,1024]{1,0:T(8,128)}, f32[64,1024]{1,0:T(8,128)}, f32[64,1024]{1,0:T(8,128)}, f32[1024]{0:T(1024)S(1)}, /*index=5*/f32[1024]{...) while((s32[]{:T(128)}, f32[64,1024]{1,0:T(8,128)}, ...), condition=%wide.region_27.28_spmd.clone.clone.clone, body=%wide.region_12.27_spmd.clone.clone.clone.sunk | while | flops 410291200 | bytes 27419500 | solution.py:75
  360.0 2.1 dynamic-slice_bitcast_fusion.22
  362.9 2.5 multiply_reduce_fusion.29
  369.2 2.2 bitcast_dynamic-update-slice_fusion.17
  375.0 2.1 dynamic-slice_bitcast_fusion.22
  377.9 2.5 multiply_reduce_fusion.29
  386.1 2.2 bitcast_dynamic-update-slice_fusion.17
  394.7 2.5 multiply_reduce_fusion.29
  403.0 2.2 bitcast_dynamic-update-slice_fusion.17
  411.6 2.5 multiply_reduce_fusion.29
  419.9 2.2 bitcast_dynamic-update-slice_fusion.17
  423.3 7.0 all-gather.3
  446.0 2.7 multiply_add_fusion.4
  459.7 2.5 copy.267
  462.4 5.5 fusion.73
  469.9 2.2 convert_element_type.345
  477.2 3.3 pad_maximum_fusion
  481.7 2.5 copy.259
  500.7 3.1 add_convert_fusion.2
  507.2 17.9 %collective-permute-done.5 = bf16[2,4,104,512]{3,2,1,0:T(8,128)(2,1)S(1)} collective-permute-done((bf16[2,4,104,512]{3,2,1,0:T(8,128)(2,1)S(1)}, bf16[2,4,104,512]{3,2,1,0:T(8,128)(2,1)S(1)}, u32[]{:S(2)}, u32[]{:S(2)}) %collective-permute-start.5) | collective-permute-done | bytes 852000 | tf_op jit(solution)/shard_map/ppermute | solution.py:129
  525.4 2.1 collective-permute-start.6
  528.5 8.2 %collective-permute-done.6 = bf16[4,104,512]{2,1,0:T(8,128)(2,1)S(1)} collective-permute-done((bf16[4,104,512]{2,1,0:T(8,128)(2,1)S(1)}, bf16[4,104,512]{2,1,0:T(8,128)(2,1)S(1)}, u32[]{:S(2)}, u32[]{:S(2)}) %collective-permute-start.6) | collective-permute-done | bytes 426016 | tf_op jit(solution)/shard_map/ppermute | solution.py:129
  540.4 2.2 collective-permute-start.9
  545.9 11.5 %collective-permute-done.10 = bf16[104,1024]{1,0:T(8,128)(2,1)S(1)} collective-permute-done((bf16[104,1024]{1,0:T(8,128)(2,1)S(1)}, bf16[104,1024]{1,0:T(8,128)(2,1)S(1)}, u32[]{:S(2)}, u32[]{:S(2)}) %collective-permute-start.10) | collective-permute-done | bytes 213024 | tf_op jit(solution)/shard_map/ppermute | solution.py:129
  557.5 2.3 copy-done.48
  559.8 6.5 add_convert_fusion
  570.8 7.1 %add_convert_fusion.1 = bf16[2,4,2,160,1024]{4,3,1,2,0:T(8,128)(2,1)S(1)} fusion(bf16[2,4,2,160,1024]{4,3,1,2,0:T(8,128)(2,1)} %collective-permute-done.12, bf16[2,4,2,160,1024]{4,3,1,2,0:T(8,128)(2,1)} %copy-done.47), kind=kLoop, calls=%fused_computation.106 | loop fusion | flops 10485760 | bytes 15728640 | tf_op jit(solution)/shard_map/convert_element_type | solution.py:133
  582.2 17.8 %collective-permute-done.21 = bf16[2,4,160,512]{3,2,1,0:T(8,128)(2,1)S(1)} collective-permute-done((bf16[2,4,160,512]{3,2,1,0:T(8,128)(2,1)}, bf16[2,4,160,512]{3,2,1,0:T(8,128)(2,1)S(1)}, u32[]{:S(2)}, u32[]{:S(2)}) %collective-permute-start.21) | collective-permute-done | bytes 1310752 | tf_op jit(solution)/shard_map/ppermute | solution.py:129
  603.7 24.3 %collective-permute-done.13 = bf16[2,4,160,512]{3,2,1,0:T(8,128)(2,1)S(1)} collective-permute-done((bf16[2,4,160,512]{3,2,1,0:T(8,128)(2,1)S(1)}, bf16[2,4,160,512]{3,2,1,0:T(8,128)(2,1)S(1)}, u32[]{:S(2)}, u32[]{:S(2)}) %collective-permute-start.13) | collective-permute-done | bytes 1310752 | tf_op jit(solution)/shard_map/ppermute | solution.py:129
  631.8 12.0 %collective-permute-done.22 = bf16[4,160,512]{2,1,0:T(8,128)(2,1)S(1)} collective-permute-done((bf16[4,160,512]{2,1,0:T(8,128)(2,1)S(1)}, bf16[4,160,512]{2,1,0:T(8,128)(2,1)S(1)}, u32[]{:S(2)}, u32[]{:S(2)}) %collective-permute-start.22) | collective-permute-done | bytes 655392 | tf_op jit(solution)/shard_map/ppermute | solution.py:129
  644.4 2.6 collective-permute-start.26
  649.0 4.7 collective-permute-done.14
  656.1 3.7 collective-permute-start.18
  659.9 8.8 %collective-permute-start.17 = (bf16[160,1024]{1,0:T(8,128)(2,1)S(1)}, bf16[160,1024]{1,0:T(8,128)(2,1)S(1)}, u32[]{:S(2)}, u32[]{:S(2)}) collective-permute-start(bf16[160,1024]{1,0:T(8,128)(2,1)S(1)} %get-tuple-element.1182), channel_id=1, source_target_pairs={{0,2},{2,4},{4,6},{6,0},{1,3},{3,5},{5,7},{7,1},{8,10},{10,12},{12... | collective-permute-start | bytes 983048 | tf_op jit(solution)/shard_map/ppermute | solution.py:129
  669.3 21.4 %collective-permute-done.26 = bf16[160,1024]{1,0:T(8,128)(2,1)S(1)} collective-permute-done((bf16[160,1024]{1,0:T(8,128)(2,1)S(1)}, bf16[160,1024]{1,0:T(8,128)(2,1)S(1)}, u32[]{:S(2)}, u32[]{:S(2)}) %collective-permute-start.26) | collective-permute-done | bytes 327712 | tf_op jit(solution)/shard_map/ppermute | solution.py:129
  692.4 9.2 %collective-permute-done.18 = bf16[160,1024]{1,0:T(8,128)(2,1)S(1)} collective-permute-done((bf16[160,1024]{1,0:T(8,128)(2,1)S(1)}, bf16[160,1024]{1,0:T(8,128)(2,1)S(1)}, u32[]{:S(2)}, u32[]{:S(2)}) %collective-permute-start.18) | collective-permute-done | bytes 327712 | tf_op jit(solution)/shard_map/ppermute | solution.py:129
  (605 shorter events, 192.4 us)
Async XLA Ops:
  7.2 16.9 %copy-start.5 = (bf16[2,256,1024]{2,1,0:T(8,128)(2,1)S(1)}, bf16[2,256,1024]{2,1,0:T(8,128)(2,1)}, u32[]{:S(2)}) copy-start(bf16[2,256,1024]{2,1,0:T(8,128)(2,1)} %param.25) | copy-start | bytes 3145732
  7.2 83.7 %all-gather.7.cloned.1.call-start = ((), (), s32[]{:S(2)}) async-start(), calls=%async_computation | async-start | bytes 7028736 | tf_op jit(solution)/shard_map/all_gather | solution.py:194
  16.4 211.0 %all-gather.9.cloned.1.call-start = ((), (), s32[]{:S(2)}) async-start(), calls=%async_computation.1 | async-start | bytes 21626880 | tf_op jit(solution)/shard_map/all_gather | solution.py:197
  23.6 72.4 %copy-start.108 = (f32[256]{0:T(256)}, f32[256]{0:T(256)S(1)}, u32[]{:S(2)}) copy-start(f32[256]{0:T(256)S(1)} %iota_subtract_fusion) | copy-start | bytes 3076
  24.3 79.2 %copy-start.84 = (f32[2,256]{1,0:T(2,128)}, f32[2,256]{1,0:T(2,128)S(1)}, u32[]{:S(2)}) copy-start(f32[2,256]{1,0:T(2,128)S(1)} %broadcast_multiply_fusion.9) | copy-start | bytes 6148
  24.8 78.7 %copy-start.94 = (f32[2,256]{1,0:T(2,128)}, f32[2,256]{1,0:T(2,128)S(1)}, u32[]{:S(2)}) copy-start(f32[2,256]{1,0:T(2,128)S(1)} %add_rsqrt_fusion.1) | copy-start | bytes 6148
  92.9 10.7 %copy-start.90 = (f32[1024]{0:T(1024)}, f32[1024]{0:T(1024)S(1)}, u32[]{:S(2)}) copy-start(f32[1024]{0:T(1024)S(1)} %mul.1140) | copy-start | bytes 12292
  93.0 10.6 %copy-start.92 = (f32[1024]{0:T(1024)}, f32[1024]{0:T(1024)S(1)}, u32[]{:S(2)}) copy-start(f32[1024]{0:T(1024)S(1)} %mul.1132) | copy-start | bytes 12292
  93.0 10.6 %copy-start.86 = (f32[1024]{0:T(1024)}, f32[1024]{0:T(1024)S(1)}, u32[]{:S(2)}) copy-start(f32[1024]{0:T(1024)S(1)} %add.462) | copy-start | bytes 12292
  93.1 10.5 %copy-start.80 = (f32[1024]{0:T(1024)}, f32[1024]{0:T(1024)S(1)}, u32[]{:S(2)}) copy-start(f32[1024]{0:T(1024)S(1)} %mul.1118) | copy-start | bytes 12292
  93.5 10.1 %copy-start.7 = (f32[2,256,1024]{2,1,0:T(8,128)}, f32[2,256,1024]{2,1,0:T(8,128)S(1)}, u32[]{:S(2)}) copy-start(f32[2,256,1024]{2,1,0:T(8,128)S(1)} %fusion.68) | copy-start | bytes 6291460
  93.6 10.0 %collective-permute-start = (f32[2,1024]{1,0:T(2,128)S(1)}, f32[2,1024]{1,0:T(2,128)S(1)}, u32[]{:S(2)}, u32[]{:S(2)}) collective-permute-start(f32[2,1024]{1,0:T(2,128)S(1)} %bitcast.564), channel_id=1, source_target_pairs={{0,8},{8,16},{16,24},{1,9},{9,17},{17,25},{2,10},{10,18},{18,26},{... | collective-permute-start | bytes 24584 | tf_op jit(solution)/shard_map/ppermute | solution.py:93
  95.8 7.8 %copy-start.88 = (f32[1024]{0:T(1024)}, f32[1024]{0:T(1024)S(1)}, u32[]{:S(2)}) copy-start(f32[1024]{0:T(1024)S(1)} %mul.1121) | copy-start | bytes 12292
  95.9 7.8 %copy-start.100 = (f32[1024]{0:T(1024)}, f32[1024]{0:T(1024)S(1)}, u32[]{:S(2)}) copy-start(f32[1024]{0:T(1024)S(1)} %get-tuple-element.1227) | copy-start | bytes 12292
  95.9 7.8 %copy-start.102 = (f32[1024]{0:T(1024)}, f32[1024]{0:T(1024)S(1)}, u32[]{:S(2)}) copy-start(f32[1024]{0:T(1024)S(1)} %get-tuple-element.1228) | copy-start | bytes 12292
  95.9 24.0 %copy-start.96 = (f32[1024]{0:T(1024)}, f32[1024]{0:T(1024)S(1)}, u32[]{:S(2)}) copy-start(f32[1024]{0:T(1024)S(1)} %get-tuple-element.1216) | copy-start | bytes 12292
  95.9 24.0 %copy-start.97 = (f32[1024]{0:T(1024)}, f32[1024]{0:T(1024)S(1)}, u32[]{:S(2)}) copy-start(f32[1024]{0:T(1024)S(1)} %get-tuple-element.1217) | copy-start | bytes 12292
  227.4 9.2 %copy-start.111 = (bf16[2,256,1024]{2,1,0:T(8,128)(2,1)S(1)}, bf16[2,256,1024]{2,1,0:T(8,128)(2,1)}, u32[]{:S(2)}) copy-start(bf16[2,256,1024]{2,1,0:T(8,128)(2,1)} %get-tuple-element.1219) | copy-start | bytes 3145732
  241.0 11.8 %collective-permute-start.1 = (f32[2,1024]{1,0:T(2,128)S(1)}, f32[2,1024]{1,0:T(2,128)S(1)}, u32[]{:S(2)}, u32[]{:S(2)}) collective-permute-start(f32[2,1024]{1,0:T(2,128)S(1)} %bitcast.567), channel_id=1, source_target_pairs={{0,8},{8,16},{16,24},{1,9},{9,17},{17,25},{2,10},{10,18},{18,26},{... | collective-permute-start | bytes 24584 | tf_op jit(solution)/shard_map/ppermute | solution.py:93
  244.4 8.5 %copy-start.3 = (f32[2,256,1024]{2,1,0:T(8,128)S(1)}, f32[2,256,1024]{2,1,0:T(8,128)}, u32[]{:S(2)}) copy-start(f32[2,256,1024]{2,1,0:T(8,128)} %copy-done.2) | copy-start | bytes 6291460
  252.8 13.3 %slice-start.2 = ((s8[8388608]{0:T(1024)(128)(4,1)}), s8[4194304]{0:T(1024)(128)(4,1)S(1)}, s32[]{:S(2)}) async-start(s8[8388608]{0:T(1024)(128)(4,1)} %bitcast.507), calls=%async_computation.4 | async-start | bytes 8388608
  255.9 10.2 %copy-start.74 = (bf16[2,256,1024]{2,1,0:T(8,128)(2,1)}, bf16[2,256,1024]{2,1,0:T(8,128)(2,1)S(1)}, u32[]{:S(2)}) copy-start(bf16[2,256,1024]{2,1,0:T(8,128)(2,1)S(1)} %get-tuple-element.1147) | copy-start | bytes 3145732
  256.0 10.1 %slice-start.3 = ((s8[8388608]{0:T(1024)(128)(4,1)}), s8[4194304]{0:T(1024)(128)(4,1)S(1)}, s32[]{:S(2)}) async-start(s8[8388608]{0:T(1024)(128)(4,1)} %bitcast.507), calls=%async_computation.5 | async-start | bytes 8388608
  266.1 7.6 %copy-start.29 = (bf16[32,32,1024]{2,1,0:T(8,128)(2,1)S(1)}, bf16[32,32,1024]{2,1,0:T(8,128)(2,1)}, u32[]{:S(2)}) copy-start(bf16[32,32,1024]{2,1,0:T(8,128)(2,1)} %get-tuple-element.1130) | copy-start | bytes 6291460
  277.5 12.9 %copy-start.62 = (bf16[32,32,1024]{2,1,0:T(8,128)(2,1)S(1)}, bf16[32,32,1024]{2,1,0:T(8,128)(2,1)}, u32[]{:S(2)}) copy-start(bf16[32,32,1024]{2,1,0:T(8,128)(2,1)} %get-tuple-element.1126) | copy-start | bytes 6291460
  277.5 12.9 %copy-start.63 = (bf16[32,32,1024]{2,1,0:T(8,128)(2,1)S(1)}, bf16[32,32,1024]{2,1,0:T(8,128)(2,1)}, u32[]{:S(2)}) copy-start(bf16[32,32,1024]{2,1,0:T(8,128)(2,1)} %get-tuple-element.1127) | copy-start | bytes 6291460
  277.6 12.9 %copy-start.64 = (bf16[32,32,1024]{2,1,0:T(8,128)(2,1)S(1)}, bf16[32,32,1024]{2,1,0:T(8,128)(2,1)}, u32[]{:S(2)}) copy-start(bf16[32,32,1024]{2,1,0:T(8,128)(2,1)} %get-tuple-element.1128) | copy-start | bytes 6291460
  290.5 7.7 %copy-start.75 = (bf16[2,256,1024]{2,1,0:T(8,128)(2,1)S(1)}, bf16[2,256,1024]{2,1,0:T(8,128)(2,1)}, u32[]{:S(2)}) copy-start(bf16[2,256,1024]{2,1,0:T(8,128)(2,1)} %copy-done.74) | copy-start | bytes 3145732
  290.5 7.7 %copy-start.113 = (bf16[2,256,4096]{2,1,0:T(8,128)(2,1)S(1)}, bf16[2,256,4096]{2,1,0:T(8,128)(2,1)}, u32[]{:S(2)}) copy-start(bf16[2,256,4096]{2,1,0:T(8,128)(2,1)} %multiply_convert_fusion) | copy-start | bytes 12582916
  298.2 18.0 %copy-start.27 = (f32[2,256,1024]{2,1,0:T(8,128)}, f32[2,256,1024]{2,1,0:T(8,128)S(1)}, u32[]{:S(2)}) copy-start(f32[2,256,1024]{2,1,0:T(8,128)S(1)} %fusion.56) | copy-start | bytes 6291460
  305.2 8.3 %copy-start.76 = (bf16[2,256,1024]{2,1,0:T(8,128)(2,1)S(1)}, bf16[2,256,1024]{2,1,0:T(8,128)(2,1)}, u32[]{:S(2)}) copy-start(bf16[2,256,1024]{2,1,0:T(8,128)(2,1)} %get-tuple-element.1149) | copy-start | bytes 3145732
  313.5 9.4 %slice-start = ((s8[8388608]{0:T(1024)(128)(4,1)}), s8[4194304]{0:T(1024)(128)(4,1)S(1)}, s32[]{:S(2)}) async-start(s8[8388608]{0:T(1024)(128)(4,1)} %bitcast.503), calls=%async_computation.2 | async-start | bytes 8388608
  321.6 21.9 %collective-permute-start.2 = (f32[2,1024]{1,0:T(2,128)S(1)}, f32[2,1024]{1,0:T(2,128)S(1)}, u32[]{:S(2)}, u32[]{:S(2)}) collective-permute-start(f32[2,1024]{1,0:T(2,128)S(1)} %bitcast.565), channel_id=1, source_target_pairs={{8,0},{16,8},{24,16},{9,1},{17,9},{25,17},{10,2},{18,10},{26,18},{... | collective-permute-start | bytes 24584 | tf_op jit(solution)/shard_map/ppermute | solution.py:93
  357.6 73.4 %copy-start.79 = (f32[2,2,1024]{2,1,0:T(2,128)S(1)}, f32[2,2,1024]{2,1,0:T(2,128)}, u32[]{:S(2)}) copy-start(f32[2,2,1024]{2,1,0:T(2,128)} %copy-done.78) | copy-start | bytes 49156
  448.8 13.4 %collective-permute-start.3 = (f32[2,1024]{1,0:T(2,128)S(1)}, f32[2,1024]{1,0:T(2,128)S(1)}, u32[]{:S(2)}, u32[]{:S(2)}) collective-permute-start(f32[2,1024]{1,0:T(2,128)S(1)} %bitcast.562), channel_id=1, source_target_pairs={{8,0},{16,8},{24,16},{9,1},{17,9},{25,17},{10,2},{18,10},{26,18},{... | collective-permute-start | bytes 24584 | tf_op jit(solution)/shard_map/ppermute | solution.py:93
  454.5 7.7 %copy-start.91 = (f32[1024]{0:T(1024)S(1)}, f32[1024]{0:T(1024)}, u32[]{:S(2)}) copy-start(f32[1024]{0:T(1024)} %copy-done.90) | copy-start | bytes 12292
  454.5 7.7 %copy-start.93 = (f32[1024]{0:T(1024)S(1)}, f32[1024]{0:T(1024)}, u32[]{:S(2)}) copy-start(f32[1024]{0:T(1024)} %copy-done.92) | copy-start | bytes 12292
  475.5 25.2 %collective-permute-start.4 = (bf16[2,4,2,104,1024]{4,3,1,2,0:T(8,128)(2,1)}, bf16[2,4,2,104,1024]{4,3,1,2,0:T(8,128)(2,1)}, u32[]{:S(2)}, u32[]{:S(2)}) collective-permute-start(bf16[2,4,2,104,1024]{4,3,1,2,0:T(8,128)(2,1)} %pad_maximum_fusion.1), channel_id=1, source_target_pairs={{0,8},{8,0},{1,9},{9,1},{2,10},{10,2},{3,11},{11,3},{4,12},{12,4},... | collective-permute-start | bytes 10223624 | tf_op jit(solution)/shard_map/ppermute | solution.py:129
  480.5 77.0 %collective-permute-start.20 = (bf16[2,4,2,160,1024]{4,3,1,2,0:T(8,128)(2,1)}, bf16[2,4,2,160,1024]{4,3,1,2,0:T(8,128)(2,1)S(1)}, u32[]{:S(2)}, u32[]{:S(2)}) collective-permute-start(bf16[2,4,2,160,1024]{4,3,1,2,0:T(8,128)(2,1)} %pad_maximum_fusion), channel_id=1, source_target_pairs={{0,8},{8,0},{1,9},{9,1},{2,10},{10,2},{3,11},{11,3},{4,12},{12,4},... | collective-permute-start | bytes 15728648 | tf_op jit(solution)/shard_map/ppermute | solution.py:129
  499.7 71.2 %collective-permute-start.12 = (bf16[2,4,2,160,1024]{4,3,1,2,0:T(8,128)(2,1)}, bf16[2,4,2,160,1024]{4,3,1,2,0:T(8,128)(2,1)}, u32[]{:S(2)}, u32[]{:S(2)}) collective-permute-start(bf16[2,4,2,160,1024]{4,3,1,2,0:T(8,128)(2,1)} %bitcast_dynamic-update-slice_fusion.4), channel_id=1, source_target_pairs={{0,8},{8,0},{1,9},{9,1},{2,10},{10,2},{3,11},{11,3},{4,12},{12,4},... | collective-permute-start | bytes 15728648 | tf_op jit(solution)/shard_map/ppermute | solution.py:129
  504.2 20.9 %collective-permute-start.5 = (bf16[2,4,104,512]{3,2,1,0:T(8,128)(2,1)S(1)}, bf16[2,4,104,512]{3,2,1,0:T(8,128)(2,1)S(1)}, u32[]{:S(2)}, u32[]{:S(2)}) collective-permute-start(bf16[2,4,104,512]{3,2,1,0:T(8,128)(2,1)S(1)} %dynamic-slice_bitcast_fusion.10), channel_id=1, source_target_pairs={{0,1},{1,0},{2,3},{3,2},{4,5},{5,4},{6,7},{7,6},{8,9},{9,8},{10,11... | collective-permute-start | bytes 2555912 | tf_op jit(solution)/shard_map/ppermute | solution.py:129
  505.0 22.5 %collective-permute-start.7 = (bf16[4,2,104,512]{3,2,0,1:T(8,128)(2,1)S(1)}, bf16[4,2,104,512]{3,2,0,1:T(8,128)(2,1)S(1)}, u32[]{:S(2)}, u32[]{:S(2)}) collective-permute-start(bf16[4,2,104,512]{3,2,0,1:T(8,128)(2,1)S(1)} %dynamic-slice_bitcast_fusion.9), channel_id=1, source_target_pairs={{0,16},{16,0},{1,17},{17,1},{2,18},{18,2},{3,19},{19,3},{4,20},{20... | collective-permute-start | bytes 2555912 | tf_op jit(solution)/shard_map/ppermute | solution.py:129
  507.2 20.6 %copy-start.47 = (bf16[2,4,2,160,1024]{4,3,1,2,0:T(8,128)(2,1)}, bf16[2,4,2,160,1024]{4,3,1,2,0:T(8,128)(2,1)S(1)}, u32[]{:S(2)}) copy-start(bf16[2,4,2,160,1024]{4,3,1,2,0:T(8,128)(2,1)S(1)} %bitcast_dynamic-update-slice_fusion.9) | copy-start | bytes 15728644
  525.4 11.3 %collective-permute-start.6 = (bf16[4,104,512]{2,1,0:T(8,128)(2,1)S(1)}, bf16[4,104,512]{2,1,0:T(8,128)(2,1)S(1)}, u32[]{:S(2)}, u32[]{:S(2)}) collective-permute-start(bf16[4,104,512]{2,1,0:T(8,128)(2,1)S(1)} %dynamic-slice_bitcast_fusion.16), channel_id=1, source_target_pairs={{0,16},{16,0},{1,17},{17,1},{2,18},{18,2},{3,19},{19,3},{4,20},{20... | collective-permute-start | bytes 1277960 | tf_op jit(solution)/shard_map/ppermute | solution.py:129
  527.8 14.7 %copy-start.39 = (f32[2,256,1024]{2,1,0:T(8,128)S(1)}, f32[2,256,1024]{2,1,0:T(8,128)}, u32[]{:S(2)}) copy-start(f32[2,256,1024]{2,1,0:T(8,128)} %get-tuple-element.1102) | copy-start | bytes 6291460
  527.9 10.7 %collective-permute-start.8 = (bf16[4,104,512]{2,1,0:T(8,128)(2,1)S(1)}, bf16[4,104,512]{2,1,0:T(8,128)(2,1)S(1)}, u32[]{:S(2)}, u32[]{:S(2)}) collective-permute-start(bf16[4,104,512]{2,1,0:T(8,128)(2,1)S(1)} %dynamic-slice_bitcast_fusion.15), channel_id=1, source_target_pairs={{0,1},{1,0},{2,3},{3,2},{4,5},{5,4},{6,7},{7,6},{8,9},{9,8},{10,11... | collective-permute-start | bytes 1277960 | tf_op jit(solution)/shard_map/ppermute | solution.py:129
  538.7 7.1 %collective-permute-start.11 = (bf16[104,1024]{1,0:T(8,128)(2,1)S(1)}, bf16[104,1024]{1,0:T(8,128)(2,1)S(1)}, u32[]{:S(2)}, u32[]{:S(2)}) collective-permute-start(bf16[104,1024]{1,0:T(8,128)(2,1)S(1)} %get-tuple-element.1187), channel_id=1, source_target_pairs={{0,6},{2,0},{4,2},{6,4},{1,7},{3,1},{5,3},{7,5},{8,14},{10,8},{12,... | collective-permute-start | bytes 638984 | tf_op jit(solution)/shard_map/ppermute | solution.py:129
  540.2 17.2 %collective-permute-start.10 = (bf16[104,1024]{1,0:T(8,128)(2,1)S(1)}, bf16[104,1024]{1,0:T(8,128)(2,1)S(1)}, u32[]{:S(2)}, u32[]{:S(2)}) collective-permute-start(bf16[104,1024]{1,0:T(8,128)(2,1)S(1)} %get-tuple-element.1186), channel_id=1, source_target_pairs={{0,4},{2,6},{4,0},{6,2},{1,5},{3,7},{5,1},{7,3},{8,12},{10,14},{12... | collective-permute-start | bytes 638984 | tf_op jit(solution)/shard_map/ppermute | solution.py:129
  540.4 17.0 %collective-permute-start.9 = (bf16[104,1024]{1,0:T(8,128)(2,1)S(1)}, bf16[104,1024]{1,0:T(8,128)(2,1)S(1)}, u32[]{:S(2)}, u32[]{:S(2)}) collective-permute-start(bf16[104,1024]{1,0:T(8,128)(2,1)S(1)} %get-tuple-element.1185), channel_id=1, source_target_pairs={{0,2},{2,4},{4,6},{6,0},{1,3},{3,5},{5,7},{7,1},{8,10},{10,12},{12... | collective-permute-start | bytes 638984 | tf_op jit(solution)/shard_map/ppermute | solution.py:129
  568.1 31.9 %collective-permute-start.21 = (bf16[2,4,160,512]{3,2,1,0:T(8,128)(2,1)}, bf16[2,4,160,512]{3,2,1,0:T(8,128)(2,1)S(1)}, u32[]{:S(2)}, u32[]{:S(2)}) collective-permute-start(bf16[2,4,160,512]{3,2,1,0:T(8,128)(2,1)} %dynamic-slice_bitcast_fusion.6), channel_id=1, source_target_pairs={{0,1},{1,0},{2,3},{3,2},{4,5},{5,4},{6,7},{7,6},{8,9},{9,8},{10,11... | collective-permute-start | bytes 3932168 | tf_op jit(solution)/shard_map/ppermute | solution.py:129
  569.8 31.9 %collective-permute-start.23 = (bf16[4,2,160,512]{3,2,0,1:T(8,128)(2,1)}, bf16[4,2,160,512]{3,2,0,1:T(8,128)(2,1)S(1)}, u32[]{:S(2)}, u32[]{:S(2)}) collective-permute-start(bf16[4,2,160,512]{3,2,0,1:T(8,128)(2,1)} %dynamic-slice_bitcast_fusion.5), channel_id=1, source_target_pairs={{0,16},{16,0},{1,17},{17,1},{2,18},{18,2},{3,19},{19,3},{4,20},{20... | collective-permute-start | bytes 3932168 | tf_op jit(solution)/shard_map/ppermute | solution.py:129
  578.7 21.3 %copy-start.20 = (bf16[2,4,2,160,512]{4,3,1,2,0:T(8,128)(2,1)S(1)}, bf16[2,4,2,160,512]{4,3,1,2,0:T(8,128)(2,1)}, u32[]{:S(2)}) copy-start(bf16[2,4,2,160,512]{4,3,1,2,0:T(8,128)(2,1)} %copy-done.19) | copy-start | bytes 7864324
  578.7 49.4 %collective-permute-start.13 = (bf16[2,4,160,512]{3,2,1,0:T(8,128)(2,1)S(1)}, bf16[2,4,160,512]{3,2,1,0:T(8,128)(2,1)S(1)}, u32[]{:S(2)}, u32[]{:S(2)}) collective-permute-start(bf16[2,4,160,512]{3,2,1,0:T(8,128)(2,1)S(1)} %dynamic-slice_bitcast_fusion.8), channel_id=1, source_target_pairs={{0,1},{1,0},{2,3},{3,2},{4,5},{5,4},{6,7},{7,6},{8,9},{9,8},{10,11... | collective-permute-start | bytes 3932168 | tf_op jit(solution)/shard_map/ppermute | solution.py:129
  580.5 49.3 %collective-permute-start.15 = (bf16[4,2,160,512]{3,2,0,1:T(8,128)(2,1)S(1)}, bf16[4,2,160,512]{3,2,0,1:T(8,128)(2,1)S(1)}, u32[]{:S(2)}, u32[]{:S(2)}) collective-permute-start(bf16[4,2,160,512]{3,2,0,1:T(8,128)(2,1)S(1)} %dynamic-slice_bitcast_fusion.7), channel_id=1, source_target_pairs={{0,16},{16,0},{1,17},{17,1},{2,18},{18,2},{3,19},{19,3},{4,20},{20... | collective-permute-start | bytes 3932168 | tf_op jit(solution)/shard_map/ppermute | solution.py:129
  600.4 43.4 %collective-permute-start.22 = (bf16[4,160,512]{2,1,0:T(8,128)(2,1)S(1)}, bf16[4,160,512]{2,1,0:T(8,128)(2,1)S(1)}, u32[]{:S(2)}, u32[]{:S(2)}) collective-permute-start(bf16[4,160,512]{2,1,0:T(8,128)(2,1)S(1)} %dynamic-slice_bitcast_fusion.12), channel_id=1, source_target_pairs={{0,16},{16,0},{1,17},{17,1},{2,18},{18,2},{3,19},{19,3},{4,20},{20... | collective-permute-start | bytes 1966088 | tf_op jit(solution)/shard_map/ppermute | solution.py:129
  602.2 41.9 %collective-permute-start.24 = (bf16[4,160,512]{2,1,0:T(8,128)(2,1)S(1)}, bf16[4,160,512]{2,1,0:T(8,128)(2,1)S(1)}, u32[]{:S(2)}, u32[]{:S(2)}) collective-permute-start(bf16[4,160,512]{2,1,0:T(8,128)(2,1)S(1)} %dynamic-slice_bitcast_fusion.11), channel_id=1, source_target_pairs={{0,1},{1,0},{2,3},{3,2},{4,5},{5,4},{6,7},{7,6},{8,9},{9,8},{10,11... | collective-permute-start | bytes 1966088 | tf_op jit(solution)/shard_map/ppermute | solution.py:129
  628.5 25.1 %collective-permute-start.14 = (bf16[4,160,512]{2,1,0:T(8,128)(2,1)S(1)}, bf16[4,160,512]{2,1,0:T(8,128)(2,1)S(1)}, u32[]{:S(2)}, u32[]{:S(2)}) collective-permute-start(bf16[4,160,512]{2,1,0:T(8,128)(2,1)S(1)} %dynamic-slice_bitcast_fusion.14), channel_id=1, source_target_pairs={{0,16},{16,0},{1,17},{17,1},{2,18},{18,2},{3,19},{19,3},{4,20},{20... | collective-permute-start | bytes 1966088 | tf_op jit(solution)/shard_map/ppermute | solution.py:129
  630.3 23.5 %collective-permute-start.16 = (bf16[4,160,512]{2,1,0:T(8,128)(2,1)S(1)}, bf16[4,160,512]{2,1,0:T(8,128)(2,1)S(1)}, u32[]{:S(2)}, u32[]{:S(2)}) collective-permute-start(bf16[4,160,512]{2,1,0:T(8,128)(2,1)S(1)} %dynamic-slice_bitcast_fusion.13), channel_id=1, source_target_pairs={{0,1},{1,0},{2,3},{3,2},{4,5},{5,4},{6,7},{7,6},{8,9},{9,8},{10,11... | collective-permute-start | bytes 1966088 | tf_op jit(solution)/shard_map/ppermute | solution.py:129
  644.4 15.5 %collective-permute-start.27 = (bf16[160,1024]{1,0:T(8,128)(2,1)S(1)}, bf16[160,1024]{1,0:T(8,128)(2,1)S(1)}, u32[]{:S(2)}, u32[]{:S(2)}) collective-permute-start(bf16[160,1024]{1,0:T(8,128)(2,1)S(1)} %get-tuple-element.1181), channel_id=1, source_target_pairs={{0,6},{2,0},{4,2},{6,4},{1,7},{3,1},{5,3},{7,5},{8,14},{10,8},{12,... | collective-permute-start | bytes 983048 | tf_op jit(solution)/shard_map/ppermute | solution.py:129
  644.4 46.3 %collective-permute-start.26 = (bf16[160,1024]{1,0:T(8,128)(2,1)S(1)}, bf16[160,1024]{1,0:T(8,128)(2,1)S(1)}, u32[]{:S(2)}, u32[]{:S(2)}) collective-permute-start(bf16[160,1024]{1,0:T(8,128)(2,1)S(1)} %get-tuple-element.1180), channel_id=1, source_target_pairs={{0,4},{2,6},{4,0},{6,2},{1,5},{3,7},{5,1},{7,3},{8,12},{10,14},{12... | collective-permute-start | bytes 983048 | tf_op jit(solution)/shard_map/ppermute | solution.py:129
  647.0 43.7 %collective-permute-start.25 = (bf16[160,1024]{1,0:T(8,128)(2,1)S(1)}, bf16[160,1024]{1,0:T(8,128)(2,1)S(1)}, u32[]{:S(2)}, u32[]{:S(2)}) collective-permute-start(bf16[160,1024]{1,0:T(8,128)(2,1)S(1)} %get-tuple-element.1179), channel_id=1, source_target_pairs={{0,2},{2,4},{4,6},{6,0},{1,3},{3,5},{5,7},{7,1},{8,10},{10,12},{12... | collective-permute-start | bytes 983048 | tf_op jit(solution)/shard_map/ppermute | solution.py:129
  654.2 38.2 %collective-permute-start.19 = (bf16[160,1024]{1,0:T(8,128)(2,1)S(1)}, bf16[160,1024]{1,0:T(8,128)(2,1)S(1)}, u32[]{:S(2)}, u32[]{:S(2)}) collective-permute-start(bf16[160,1024]{1,0:T(8,128)(2,1)S(1)} %get-tuple-element.1184), channel_id=1, source_target_pairs={{0,6},{2,0},{4,2},{6,4},{1,7},{3,1},{5,3},{7,5},{8,14},{10,8},{12,... | collective-permute-start | bytes 983048 | tf_op jit(solution)/shard_map/ppermute | solution.py:129
  656.1 45.5 %collective-permute-start.18 = (bf16[160,1024]{1,0:T(8,128)(2,1)S(1)}, bf16[160,1024]{1,0:T(8,128)(2,1)S(1)}, u32[]{:S(2)}, u32[]{:S(2)}) collective-permute-start(bf16[160,1024]{1,0:T(8,128)(2,1)S(1)} %get-tuple-element.1183), channel_id=1, source_target_pairs={{0,4},{2,6},{4,0},{6,2},{1,5},{3,7},{5,1},{7,3},{8,12},{10,14},{12... | collective-permute-start | bytes 983048 | tf_op jit(solution)/shard_map/ppermute | solution.py:129
  659.9 41.7 %collective-permute-start.17 = (bf16[160,1024]{1,0:T(8,128)(2,1)S(1)}, bf16[160,1024]{1,0:T(8,128)(2,1)S(1)}, u32[]{:S(2)}, u32[]{:S(2)}) collective-permute-start(bf16[160,1024]{1,0:T(8,128)(2,1)S(1)} %get-tuple-element.1182), channel_id=1, source_target_pairs={{0,2},{2,4},{4,6},{6,0},{1,3},{3,5},{5,7},{7,1},{8,10},{10,12},{12... | collective-permute-start | bytes 983048 | tf_op jit(solution)/shard_map/ppermute | solution.py:129
  (96 other events, 267.9 us)
Sparse Core Ops, SparseCore 0:
  16.5 74.3 all-gather.6
  94.3 133.0 all-gather.8

commit v2 on v1

v2 whole, which is shorter than its diff:
```python
import functools

import jax
import jax.numpy as jnp
from jax import lax
from jax.experimental import pallas as pl
from jax.experimental.pallas import tpu as pltpu
from jax.sharding import PartitionSpec as P

EPS = 1e-05

def norm_stats(field):
    center = field - jnp.mean(field, axis=-1, keepdims=True)
    inverse = lax.rsqrt(jnp.mean(center * center, axis=-1, keepdims=True) + EPS)
    return (center * inverse, inverse)


def norm_back(grad_normed, normalized, inverse):
    mean_grad = jnp.mean(grad_normed, axis=-1, keepdims=True)
    mean_proj = jnp.mean(grad_normed * normalized, axis=-1, keepdims=True)
    return inverse * (grad_normed - mean_grad - normalized * mean_proj)


SEQ = ("y", "core")
DP = ("z", "x")
ALL = ("y", "core", "z", "x")


def scan_tiles(rate, reverse):
    row = lax.broadcasted_iota(jnp.int32, (8, rate.shape[-1]), 0)
    steps = []
    for distance in (1, 2, 4):
        inside = row < 8 - distance if reverse else row >= distance
        steps.append((distance, jnp.where(inside, jnp.exp(-float(distance) * rate), 0.0)))
    return row, steps


def turn(x, distance, reverse):
    return pltpu.roll(x, 8 - distance if reverse else distance, 0)


def scan_rows(x, steps, reverse):
    for distance, factor in steps:
        x = x + factor * turn(x, distance, reverse)
    return x


def wkv_kernel(k_ref, v_ref, r_ref, a0_ref, b0_ref, u_ref, rate_ref, a_ref, b_ref, mixed_ref):
    seqs, span, lanes = k_ref.shape
    rate = rate_ref[...]
    boost = jnp.exp(u_ref[...])
    row, steps = scan_tiles(rate, False)
    falling = jnp.exp(-row.astype(jnp.float32) * rate)
    fall_all = jnp.exp(-8.0 * rate)
    first = row < 1
    pair = 16

    def body(i, carry):
        at = pl.ds(pl.multiple_of(i * pair, pair), pair)
        new = []
        for n in range(seqs):
            k16, v16, r16 = (ref[n, at, :] for ref in (k_ref, v_ref, r_ref))
            state = carry[2 * n : 2 * n + 2]
            tiles = []
            for g in range(2):
                k, v, r = (t[g * 8 : g * 8 + 8] for t in (k16, v16, r16))
                weight = jnp.exp(k)
                bonus = boost * weight
                sums = [scan_rows(t, steps, False) for t in (weight * v, weight)]
                a, b = (
                    falling * c + jnp.where(first, 0.0, turn(t, 1, False))
                    for c, t in zip(state, sums)
                )
                state = tuple(fall_all * c + t[7:8] for c, t in zip(state, sums))
                mixed = jax.nn.sigmoid(r) * ((a + bonus * v) / (b + bonus))
                tiles.append((a, b, mixed))
            a, b, mixed = (jnp.concatenate(t, axis=0) for t in zip(*tiles))
            a_ref[n, at, :] = a
            b_ref[n, at, :] = b
            mixed_ref[n, at, :] = mixed.astype(mixed_ref.dtype)
            new += state
        return tuple(new)

    start = []
    for n in range(seqs):
        start += [a0_ref[n : n + 1, :], b0_ref[n : n + 1, :]]
    lax.fori_loop(0, span // pair, body, tuple(start), unroll=2)


def wkv_back_kernel(
    k_ref, v_ref, r_ref, a_ref, b_ref, g_ref, p0_ref, q0_ref, u_ref, rate_ref,
    k_out, v_out, rate_out, first_out,
):
    seqs, span, lanes = k_ref.shape
    rate = rate_ref[...]
    boost = jnp.exp(u_ref[...])
    row, steps = scan_tiles(rate, True)
    falling = jnp.exp((row.astype(jnp.float32) - 7.0) * rate)
    fall_all = jnp.exp(-8.0 * rate)
    last = row > 6
    pair = 16
    count = span // pair

    def body(i, carry):
        at = pl.ds(pl.multiple_of((count - 1 - i) * pair, pair), pair)
        new = []
        rate_sum, first_sum = carry[-2:]
        for n in range(seqs):
            loaded = [ref[n, at, :] for ref in (k_ref, v_ref, r_ref, a_ref, b_ref, g_ref)]
            state = carry[2 * n : 2 * n + 2]
            tiles = []
            for g in (1, 0):
                k, v, r, a, b, grad = (t[g * 8 : g * 8 + 8] for t in loaded)
                weight = jnp.exp(k)
                bonus = boost * weight
                over = 1.0 / (b + bonus)
                wkv = (a + bonus * v) * over
                alpha = grad * jax.nn.sigmoid(r) * over
                sums = [scan_rows(t, steps, True) for t in (alpha, -alpha * wkv)]
                p, q = (
                    falling * c + jnp.where(last, 0.0, turn(t, 1, True))
                    for c, t in zip(state, sums)
                )
                state = tuple(fall_all * c + t[0:1] for c, t in zip(state, sums))
                share = alpha * bonus
                own = share * (v - wkv)
                tiles.append((own + weight * (p * v + q), share + weight * p))
                rate_sum = rate_sum + (a * p + b * q)
                first_sum = first_sum + own
            k_grad, v_grad = (jnp.concatenate(t, axis=0) for t in zip(*tiles[::-1]))
            k_out[n, at, :] = k_grad.astype(k_out.dtype)
            v_out[n, at, :] = v_grad.astype(v_out.dtype)
            new += state
        return tuple(new) + (rate_sum, first_sum)

    start = []
    for n in range(seqs):
        start += [p0_ref[n : n + 1, :], q0_ref[n : n + 1, :]]
    zero = jnp.zeros((8, lanes), jnp.float32)
    done = lax.fori_loop(0, count, body, tuple(start) + (zero, zero), unroll=2)
    rate_out[...] = -rate * jnp.exp(-rate) * jnp.sum(done[-2], axis=0, keepdims=True)
    first_out[...] = jnp.sum(done[-1], axis=0, keepdims=True)


LANES = 256


def wkv_specs(seqs, span):
    field = pl.BlockSpec((seqs, span, LANES), lambda j: (0, 0, j))
    state = pl.BlockSpec((seqs, LANES), lambda j: (0, j))
    vector = pl.BlockSpec((1, LANES), lambda j: (0, j))
    return field, state, vector


def wkv_forward(k, v, r, a0, b0, u, rate):
    seqs, span, channels = k.shape
    field, state, vector = wkv_specs(seqs, span)
    return pl.pallas_call(
        wkv_kernel,
        grid=(channels // LANES,),
        out_shape=[jax.ShapeDtypeStruct(k.shape, t) for t in (jnp.float32, jnp.float32, jnp.bfloat16)],
        in_specs=[field] * 3 + [state] * 2 + [vector] * 2,
        out_specs=[field] * 3,
        compiler_params=pltpu.CompilerParams(vmem_limit_bytes=32 << 20),
        cost_estimate=pl.CostEstimate(flops=30 * k.size, bytes_accessed=22 * k.size, transcendentals=3 * k.size),
    )(k, v, r, a0, b0, u[None], rate[None])


def wkv_backward(k, v, r, a, b, grad, p0, q0, u, rate):
    seqs, span, channels = k.shape
    field, state, vector = wkv_specs(seqs, span)
    k_grad, v_grad, decay_grad, first_grad = pl.pallas_call(
        wkv_back_kernel,
        grid=(channels // LANES,),
        out_shape=[jax.ShapeDtypeStruct(k.shape, jnp.bfloat16)] * 2
        + [jax.ShapeDtypeStruct((1, channels), jnp.float32)] * 2,
        in_specs=[field] * 6 + [state] * 2 + [vector] * 2,
        out_specs=[field] * 2 + [vector] * 2,
        compiler_params=pltpu.CompilerParams(vmem_limit_bytes=32 << 20),
        cost_estimate=pl.CostEstimate(flops=50 * k.size, bytes_accessed=28 * k.size, transcendentals=3 * k.size),
    )(k, v, r, a, b, grad, p0, q0, u[None], rate[None])
    return k_grad, v_grad, decay_grad[0], first_grad[0]


def matmul(form, left, right):
    return jnp.einsum(form, left, right, preferred_element_type=jnp.float32)


def shifted(block, axis, distance):
    count = lax.axis_size(axis)
    route = [(i - distance, i) for i in range(count) if 0 <= i - distance < count]
    return lax.ppermute(block, axis, route)


def previous_rows(field):
    came = shifted(field[:, -1, :], SEQ, 1)
    return jnp.concatenate([came[:, None, :], field[:, :-1, :]], axis=1)


def next_rows(field):
    came = shifted(field[:, 0, :], SEQ, -1)
    return jnp.concatenate([field[:, 1:, :], came[:, None, :]], axis=1)


def entering(factor, states, reverse):
    block = jnp.stack(states)
    total, power = (jnp.zeros_like(block), jnp.ones_like(factor))
    for k in range(1, lax.axis_size(SEQ)):
        total = total + power * shifted(block, SEQ, -k if reverse else k)
        power = power * factor
    return (total[0], total[1])


def after(x, deps):
    return lax.optimization_barrier((x, tuple(deps)))[0] if deps else x


def spread(block, axis):
    count = lax.axis_size(axis)
    return [
        lax.ppermute(block, axis, [(i, (i + k) % count) for i in range(count)])
        for k in range(1, count)
    ]


def beside_z(own):
    half = own.shape[1] // 2
    rows = lax.all_gather(own, "z", axis=0)
    return (rows[:, :, :half], rows[:, :, half:])


def beside_xy(pair, axes):
    return [[block] + spread(block, axis) for block, axis in zip(pair, axes)]


def other_core(parts):
    return [[spread(block, "core")[0] for block in part] for part in parts]


def assemble_kernel(entries, grid, at_ref, *refs):
    n_out = 1 + max(entry[2] for entry in entries)
    sources, outs, sems = (refs[: -n_out - 1], refs[-n_out - 1 : -1], refs[-1])
    ys, cs, zs, xs = grid
    y, c, x = (at_ref[j] for j in range(3))

    def back(at, k, count):
        return lax.rem(at - k + count, count)

    index = 0
    for dc in range(cs):
        for half, lead in enumerate((xs, ys)):
            for far in range(ys if half == 0 else xs):
                source = sources[index]
                index += 1

                def copy(k, _, source=source, dc=dc, half=half, far=far):
                    near, dz = (k // zs, lax.rem(k, zs))
                    dy, dx = (far, near) if half == 0 else (near, far)
                    block = back(y, dy, ys) * cs + back(c, dc, cs)
                    block = (block * zs + dz) * xs + back(x, dx, xs)
                    for first, rows, out, column in entries:
                        width = source.shape[-1]
                        pltpu.make_async_copy(
                            source.at[near, dz, pl.ds(first, rows), :],
                            outs[out].at[block, :, pl.ds(column + half * width, width)],
                            sems.at[out],
                        ).start()
                    return 0

                lax.fori_loop(0, lead * zs, copy, 0)
    for out in range(n_out):
        pltpu.make_async_copy(outs[out], outs[out], sems.at[out]).wait()


def assemble(mine, other, entries, shapes, grid):
    sources = [b for part in mine for b in part] + [b for part in other for b in part]
    at = jnp.stack([lax.axis_index(axis) for axis in ("y", "core", "x")]).astype(jnp.int32)
    count = grid[0] * grid[1] * grid[2] * grid[3]
    outs = pl.pallas_call(
        functools.partial(assemble_kernel, entries, grid),
        out_shape=[jax.ShapeDtypeStruct((count, *shape), jnp.bfloat16) for shape in shapes],
        in_specs=[pl.BlockSpec(memory_space=pltpu.SMEM)]
        + [pl.BlockSpec(memory_space=pl.ANY)] * len(sources),
        out_specs=[pl.BlockSpec(memory_space=pltpu.VMEM)] * len(shapes),
        scratch_shapes=[pltpu.SemaphoreType.DMA((len(shapes),))],
        compiler_params=pltpu.CompilerParams(vmem_limit_bytes=40 << 20),
    )(at, *sources)
    return [out.reshape(-1, out.shape[-1]) for out in outs]


class Partial:
    def __init__(self, parts, dim, axis, deps=(), kind=jnp.bfloat16):
        self.parts, self.dim = (parts, dim)
        self.count, self.mine = (lax.axis_size(axis), lax.axis_index(axis))
        self.sent, self.came = ([], [])
        for k in range(1, self.count):
            route = [(i, (i + k) % self.count) for i in range(self.count)]
            block = self.take(lax.rem(self.mine + k, self.count)).astype(kind)
            block = after(block, deps)
            self.sent.append(block)
            self.came.append(lax.ppermute(block, axis, route))

    def take(self, j):
        taken = [lax.dynamic_index_in_dim(p, j, self.dim, keepdims=False) for p in self.parts]
        return taken[0] if len(taken) == 1 else jnp.concatenate(taken, axis=-2)

    def finish(self, kind=jnp.bfloat16, deps=()):
        total = self.take(self.mine).astype(jnp.float32)
        for block in after(tuple(self.came), deps):
            total = total + block.astype(jnp.float32)
        return total.astype(kind)


def first_xy(parts, deps=()):
    half = parts[0].shape[-1] // 2
    a, b = ([p[..., :half] for p in parts], [p[..., half:] for p in parts])
    return (Partial(a, 2, "x", deps), Partial(b, 0, "y", deps))


def second_xy(pair, deps=(), also=()):
    a, b = (part.finish(deps=also) for part in pair)
    return (Partial([a], 0, "y", deps), Partial([b], 1, "x", deps))


def last_z(pair, also=()):
    a, b = (part.finish(deps=also) for part in pair)
    whole = jnp.concatenate([a, b], axis=-1)
    return lax.psum_scatter(whole, "z", scatter_dimension=0, tiled=False).astype(jnp.float32)


def sent(*steps):
    return [block for step in steps for block in step.sent]


def came(*steps):
    return [block for step in steps for block in step.came]


def per_device(
    tokens,
    lengths,
    cotangent,
    first_gain,
    first_bias,
    mix_key,
    mix_value,
    mix_recept,
    time_decay,
    time_first,
    key_weight,
    value_weight,
    recept_weight,
    output_weight,
    second_gain,
    second_bias,
    shift_key,
    shift_recept,
    up_weight,
    gate_weight,
    down_weight,
):
    grid = tuple(lax.axis_size(axis) for axis in ALL)
    count = grid[0] * grid[1] * grid[2] * grid[3]
    seq_count, piece_len, channels = tokens.shape
    hidden = up_weight.shape[1]
    mine = channels // count
    blocks = hidden // channels

    vectors = (
        first_gain,
        first_bias,
        mix_key,
        mix_value,
        mix_recept,
        time_decay,
        time_first,
        second_gain,
        second_bias,
        shift_key,
        shift_recept,
    )
    n_vec = len(vectors)
    packed = jnp.pad(jnp.stack(vectors), ((0, 16 - n_vec), (0, channels - mine)))
    pieces = (
        [key_weight, value_weight, recept_weight, packed],
        [output_weight] + [up_weight[:, j * channels : (j + 1) * channels] for j in range(blocks)],
        [gate_weight, down_weight],
    )
    places = (
        [(0, 0), (1, 0), (2, 0), (3, 0)],
        [(0, 0)] + [(1, j * channels) for j in range(blocks)],
        [(0, 0), (1, 0)],
    )
    chunks = [jnp.concatenate(piece) for piece in pieces]
    plans = []
    for piece, place in zip(pieces, places):
        first, entries, shapes = (0, [], {})
        for part, (out, column) in zip(piece, place):
            entries.append((first, part.shape[0], out, column))
            shapes[out] = (part.shape[0], column + channels)
            first += part.shape[0]
        plans.append((entries, [shapes[o] for o in sorted(shapes)]))
    stepwise = mine % 16 == 0

    def whole(at):
        gathered = lax.all_gather(chunks[at], ALL, axis=0)
        entries, shapes = plans[at]
        outs = []
        for out, shape in enumerate(shapes):
            cols = [gathered[:, f : f + r] for f, r, o, _ in entries if o == out]
            outs.append(jnp.concatenate(cols, axis=-1).reshape(-1, shape[1]))
        return outs

    if stepwise:
        z0 = beside_z(chunks[0])
        z1 = beside_z(after(chunks[1], z0))
        z2 = beside_z(after(chunks[2], z1))
        xy0 = beside_xy(z0, ("x", "y"))
        a0, b0 = (jnp.stack(part) for part in xy0)
        yx0 = beside_xy((a0, b0), ("y", "x"))
        xy1 = beside_xy(after(z1, yx0), ("x", "y"))
        key_mat, value_mat, recept_mat, vecs = assemble(yx0, other_core(yx0), *plans[0], grid)
    else:
        key_mat, value_mat, recept_mat, vecs = whole(0)
    vecs = vecs.reshape(count, 16, channels)[:, :n_vec, :mine]
    vecs = jnp.moveaxis(vecs, 1, 0).reshape(n_vec, channels).astype(jnp.float32)
    (
        norm_gain,
        norm_bias,
        key_mix,
        value_mix,
        recept_mix,
        decay_log,
        boost_log_scale,
        gain_two,
        bias_two,
        chan_key_mix,
        chan_recept_mix,
    ) = (vecs[j] for j in range(n_vec))
    seq_index = lax.axis_index(SEQ)
    positions = seq_index * piece_len + jnp.arange(piece_len, dtype=jnp.int32)
    live_mask = (positions[None, :] < lengths[:, None]).astype(jnp.float32)[:, :, None]
    field = tokens.astype(jnp.float32)
    normed_one, inverse_one = norm_stats(field)
    normed = normed_one * norm_gain + norm_bias
    before = previous_rows(normed)
    key_in = (normed * key_mix + before * (1.0 - key_mix)).astype(jnp.bfloat16)
    value_in = (normed * value_mix + before * (1.0 - value_mix)).astype(jnp.bfloat16)
    recept_in = (normed * recept_mix + before * (1.0 - recept_mix)).astype(jnp.bfloat16)
    lookup_matrix_output = matmul("nlc,cd->nld", key_in, key_mat)
    content_matrix_output = matmul("nlc,cd->nld", value_in, value_mat)
    recept_proj = matmul("nlc,cd->nld", recept_in, recept_mat)
    if stepwise:
        pair = after(tuple(jnp.stack(part) for part in xy1), (recept_proj, content_matrix_output))
        yx1 = beside_xy(pair, ("y", "x"))
    fading_rate_vector = jnp.exp(decay_log)
    place = jnp.arange(piece_len, dtype=jnp.float32)[:, None]
    weight = jnp.exp(lookup_matrix_output - (piece_len - 1 - place) * fading_rate_vector)
    local = (jnp.sum(weight * content_matrix_output, axis=1), jnp.sum(weight, axis=1))
    piece_fall = jnp.exp(-piece_len * fading_rate_vector)
    starting_accumulator, starting_normalizer = entering(piece_fall, local, False)
    state_a, state_b, mixed_out = wkv_forward(
        lookup_matrix_output,
        content_matrix_output,
        recept_proj,
        starting_accumulator,
        starting_normalizer,
        boost_log_scale,
        fading_rate_vector,
    )
    if stepwise:
        xy2 = beside_xy(after(z2, (yx1, mixed_out)), ("x", "y"))
        output_mat, up_mat = assemble(yx1, other_core(yx1), *plans[1], grid)
    else:
        output_mat, up_mat = whole(1)
    branch = matmul("nlc,cd->nld", mixed_out, output_mat)
    residual = field + branch
    normed_two_raw, inverse_two = norm_stats(residual)
    normed_two = normed_two_raw * gain_two + bias_two
    before_two = previous_rows(normed_two)
    ffn_key = (normed_two * chan_key_mix + before_two * (1.0 - chan_key_mix)).astype(jnp.bfloat16)
    ffn_recept = (normed_two * chan_recept_mix + before_two * (1.0 - chan_recept_mix)).astype(
        jnp.bfloat16
    )
    if stepwise:
        pair = after(tuple(jnp.stack(part) for part in xy2), (ffn_key, ffn_recept))
        yx2 = beside_xy(pair, ("y", "x"))
    up_proj = matmul("nlc,cf->nlf", ffn_key, up_mat)
    relu_up = jax.nn.relu(up_proj)
    squared = jnp.square(relu_up).astype(jnp.bfloat16)
    relu_up = relu_up.astype(jnp.bfloat16)
    if stepwise:
        gate_mat, down_mat = assemble(yx2, other_core(yx2), *plans[2], grid)
    else:
        gate_mat, down_mat = whole(2)
    down_proj = matmul("nlf,fd->nld", squared, down_mat)
    gate_value = jax.nn.sigmoid(matmul("nlc,cd->nld", ffn_recept, gate_mat))
    output = ((residual + gate_value * down_proj) * live_mask).astype(jnp.bfloat16)

    core = lax.axis_index("core")

    def outer(left, right, at):
        width = left.shape[-1] // (2 * grid[0])
        cut = [left[..., k * width : (k + 1) * width] for k in range(2 * grid[0])]
        cut = [jnp.where(at == 0, a, b) for a, b in zip(cut[::2], cut[1::2])]
        left = jnp.concatenate(cut, axis=-1)
        rows = jnp.einsum("nlc,nld->cd", left, right, preferred_element_type=jnp.float32)
        return rows.reshape(grid[0], grid[2], grid[3], -1, right.shape[-1])

    def to_core(left, right):
        send = outer(left, right, 1 - core).astype(jnp.bfloat16)
        return send, spread(send, "core")[0]

    def both_cores(left, right, came):
        return (outer(left, right, core) + came.astype(jnp.float32)).astype(jnp.bfloat16)

    def by_columns(g):
        return [g[..., j * channels : (j + 1) * channels] for j in range(g.shape[-1] // channels)]

    seed = cotangent.astype(jnp.float32) * live_mask
    down_grad = (seed * gate_value).astype(jnp.bfloat16)
    gate_grad = (seed * down_proj * gate_value * (1.0 - gate_value)).astype(jnp.bfloat16)
    down_send, down_came = to_core(squared, down_grad)
    gate_send, gate_came = to_core(ffn_recept, gate_grad)
    squared_grad = matmul("nld,fd->nlf", after(down_grad, (down_send, gate_send)), down_mat)
    up_grad = (squared_grad * 2.0 * relu_up.astype(jnp.float32)).astype(jnp.bfloat16)
    up_send, up_came = to_core(ffn_key, up_grad)
    late = (down_grad, gate_grad, down_came, gate_came)
    d_grad, g_grad, down_came, gate_came = after(late, (up_send,))
    xy1 = first_xy([both_cores(squared, d_grad, down_came), both_cores(ffn_recept, g_grad, gate_came)])
    u_grad, gate_grad, up_came = after((up_grad, gate_grad, up_came), sent(*xy1))
    ffn_key_grad = matmul("nlf,cf->nlc", u_grad, up_mat)
    ffn_recept_grad = matmul("nld,cd->nlc", gate_grad, gate_mat)
    u_grad, up_came = after((u_grad, up_came), (ffn_key_grad, ffn_recept_grad))
    grad_up_part = by_columns(both_cores(ffn_key, u_grad, up_came))
    normed_two_grad = (
        ffn_key_grad * chan_key_mix
        + ffn_recept_grad * chan_recept_mix
        + next_rows(ffn_key_grad * (1.0 - chan_key_mix) + ffn_recept_grad * (1.0 - chan_recept_mix))
    )
    gap_two = normed_two - before_two
    grad_chan_key = jnp.sum(ffn_key_grad * gap_two, axis=(0, 1))
    grad_chan_recept = jnp.sum(ffn_recept_grad * gap_two, axis=(0, 1))
    grad_gain_two = jnp.sum(normed_two_grad * normed_two_raw, axis=(0, 1))
    grad_bias_two = jnp.sum(normed_two_grad, axis=(0, 1))
    residual_grad = seed + norm_back(normed_two_grad * gain_two, normed_two_raw, inverse_two)
    branch_grad = residual_grad.astype(jnp.bfloat16)
    yx1 = second_xy(xy1, also=(branch_grad,))
    branch_grad = after(branch_grad, sent(*yx1))
    mixed_grad = matmul("nld,cd->nlc", branch_grad, output_mat)
    out_send, out_came = to_core(mixed_out, branch_grad)
    bonus = jnp.exp(boost_log_scale) * jnp.exp(lookup_matrix_output)
    over = 1.0 / (state_b + bonus)
    blended = (state_a + bonus * content_matrix_output) * over
    recept_sig = jax.nn.sigmoid(recept_proj)
    recept_grad = (mixed_grad * blended * recept_sig * (1.0 - recept_sig)).astype(jnp.bfloat16)
    alpha = mixed_grad * recept_sig * over * jnp.exp(-place * fading_rate_vector)
    local = (jnp.sum(alpha, axis=1), -jnp.sum(alpha * blended, axis=1))
    carry_p, carry_q = entering(piece_fall, local, True)
    xy2 = first_xy(grad_up_part, deps=came(*yx1))
    z1 = last_z(yx1, also=sent(*xy2))
    recept_send, recept_came = to_core(recept_in, recept_grad)
    carry_p, carry_q = after((carry_p, carry_q), sent(*xy2) + [recept_send])
    key_grad, value_grad, grad_decay, boost_adjoint_term = wkv_backward(
        lookup_matrix_output,
        content_matrix_output,
        recept_proj,
        state_a,
        state_b,
        mixed_grad,
        carry_p,
        carry_q,
        boost_log_scale,
        fading_rate_vector,
    )
    key_send, key_came = to_core(key_in, key_grad)
    value_send, value_came = to_core(value_in, value_grad)
    part_out = both_cores(mixed_out, after(branch_grad, (key_send, value_send)), out_came)
    part_recept = both_cores(recept_in, after(recept_grad, (key_send, value_send)), recept_came)
    yx2 = second_xy(xy2, also=(part_out, part_recept))
    late = (key_grad, value_grad, key_came, value_came)
    k_grad, v_grad, key_came, value_came = after(late, sent(*yx2))
    part_key = both_cores(key_in, k_grad, key_came)
    part_value = both_cores(value_in, v_grad, value_came)
    k_grad, v_grad, r_grad = after((k_grad, v_grad, recept_grad), (part_key, part_value))
    xy3 = first_xy([part_out, part_recept, part_key, part_value], deps=came(*yx2))
    z2 = last_z(yx2, also=sent(*xy3))
    k_grad, v_grad, r_grad = after((k_grad, v_grad, r_grad), sent(*xy3))
    key_in_grad = matmul("nld,cd->nlc", k_grad, key_mat)
    value_in_grad = matmul("nld,cd->nlc", v_grad, value_mat)
    recept_in_grad = matmul("nld,cd->nlc", r_grad, recept_mat)
    normed_grad = (
        key_in_grad * key_mix
        + value_in_grad * value_mix
        + recept_in_grad * recept_mix
        + next_rows(
            key_in_grad * (1.0 - key_mix)
            + value_in_grad * (1.0 - value_mix)
            + recept_in_grad * (1.0 - recept_mix)
        )
    )
    gap_one = normed - before
    grad_key_mix = jnp.sum(key_in_grad * gap_one, axis=(0, 1))
    grad_value_mix = jnp.sum(value_in_grad * gap_one, axis=(0, 1))
    grad_recept_mix = jnp.sum(recept_in_grad * gap_one, axis=(0, 1))
    grad_gain_one = jnp.sum(normed_grad * normed_one, axis=(0, 1))
    grad_bias_one = jnp.sum(normed_grad, axis=(0, 1))
    tokens_grad = residual_grad + norm_back(normed_grad * norm_gain, normed_one, inverse_one)
    sums = jnp.stack(
        [
            grad_gain_one,
            grad_bias_one,
            grad_key_mix,
            grad_value_mix,
            grad_recept_mix,
            grad_decay,
            boost_adjoint_term,
            grad_gain_two,
            grad_bias_two,
            grad_chan_key,
            grad_chan_recept,
        ]
    )
    sums = jnp.moveaxis(sums.reshape(n_vec, *grid, mine), 0, -2)
    yx3 = second_xy(xy3, also=(tokens_grad,))
    for dim, axis in ((1, "core"), (2, "x"), (0, "y"), (0, "z")):
        sums = Partial([sums], dim, axis, kind=jnp.float32).finish(jnp.float32)
    third = last_z(yx3)
    first, second = (z1, z2)
    rows_down = hidden // count
    return (
        output,
        tokens_grad,
        *(sums[j] for j in range(7)),
        third[2 * mine : 3 * mine],
        third[3 * mine :],
        third[mine : 2 * mine],
        third[:mine],
        *(sums[j] for j in range(7, n_vec)),
        jnp.concatenate([second[j * mine : (j + 1) * mine] for j in range(blocks)], axis=1),
        first[rows_down:],
        first[:rows_down],
    )


def solution(mesh):
    seq, dp = (mesh.shape["seq"], mesh.shape["dp"])
    wide = len({device.coords[0] for device in mesh.devices.reshape(-1)})
    fine = jax.sharding.Mesh(mesh.devices.reshape(seq // 2, 2, dp // wide, wide), ALL)
    field, vector, matrix = (P(DP, SEQ, None), P(ALL), P(ALL, None))
    return jax.shard_map(
        per_device,
        mesh=fine,
        in_specs=(field, P(DP), field) + (vector,) * 7 + (matrix,) * 4 + (vector,) * 4 + (matrix,) * 3,
        out_specs=(field, field) + (vector,) * 7 + (matrix,) * 4 + (vector,) * 4 + (matrix,) * 3,
        check_vma=False,
    )
```

time: 719 us -> 534 us (0.74)
  waiting for transfers between devices: 280 us -> 125 us
  local copies, waits for them, and re-layouts: 148 us -> 66.6 us
  Pallas kernels: 0 us -> 31.1 us
  starting transfers between devices: 47.6 us -> 76.5 us
  matrix products: 114 us -> 88.8 us
  blocking collectives: 13.1 us -> 22.9 us
  other arithmetic: 90.3 us -> 97.9 us
    all_gather x2, waiting for transfers between devices: 149 us -> 1.7 us  [beside_z(): rows = lax.all_gather(own, 'z', axis=0)]
    ppermute x24 -> x49, waiting for transfers between devices: 132 us -> 86.7 us  [the longest x31 65.3 us: spread(): lax.ppermute(block, axis, [(i, (i + k) % count) for i in range(count)])]
    pallas_call x0 -> x5, Pallas kernels: none -> 31.1 us  [the longest x3 20.5 us: assemble(): pl.pallas_call(functools.partial(assemble_kernel, entries, grid), out_sha...]
    dot_general x24 -> x0, matrix products: 28.5 us -> none  [the longest x12 16.5 us: one_block(): jnp.einsum('ts,nsc->ntc', strict_lower, weight, precision=lax.Precision.H...]
    ppermute x4 -> x10, waiting for transfers between devices: 0.01 us -> 25.2 us  [shifted(): return lax.ppermute(block, axis, route)]
    slice x10 -> x11, local copies, waits for them, and re-layouts: 31.4 us -> 9.4 us  [the longest x2 4.85 us: beside_z(): return (rows[:, :, :half], rows[:, :, half:])]
    ppermute x24 -> x49, starting transfers between devices: 39.9 us -> 60.6 us  [the longest x18 39.7 us: __init__(): self.came.append(lax.ppermute(block, axis, route))]
    unnamed x259 -> x276, local copies, waits for them, and re-layouts: 34.8 us -> 19.2 us
  transfers between devices with their start and end apart: 30 -> 64, of which waited for: 15 -> 22; matrix products, arithmetic and copies ran while one was open for 19% -> 41% of each run, Pallas kernels for 0% -> 5%
where the time goes in v2:
time: 534 us; the launch traced here: 525 us
  waiting for transfers between devices  125 us (23%)
  other arithmetic  97.9 us (18%)
  matrix products  88.8 us (17%)
  starting transfers between devices  76.5 us (14%)
  local copies, waits for them, and re-layouts  66.6 us (12%)
  Pallas kernels  31.1 us (6%)
  blocking collectives  22.9 us (4%)
  between operations  16.4 us (3%)
    ppermute x31, waiting for transfers between devices, spread(): lax.ppermute(block, axis, [(i, (i + k) % count) for i in range(count)])  65.3 us
    dot_general x14, matrix products, matmul(): return jnp.einsum(form, left, right, preferred_element_type=jnp.float32)  56.9 us
    ppermute x18, starting transfers between devices, __init__(): self.came.append(lax.ppermute(block, axis, route))  39.7 us
    dot_general x14, matrix products, outer(): jnp.einsum('nlc,nld->cd', left, right, preferred_element_type=jnp.float32)  31.8 us
    ppermute x10, waiting for transfers between devices, shifted(): return lax.ppermute(block, axis, route)  25.2 us
    all_gather x1, blocking collectives, beside_z(): rows = lax.all_gather(own, 'z', axis=0)  22.9 us
    ppermute x18, waiting for transfers between devices, __init__(): self.came.append(lax.ppermute(block, axis, route))  21.5 us
    ppermute x31, starting transfers between devices, spread(): lax.ppermute(block, axis, [(i, (i + k) % count) for i in range(count)])  20.9 us
  transfers between devices with their start and end apart: 64, of which 22 were waited for; matrix products, arithmetic and copies ran while one was open for 41% of the time, Pallas kernels for 5%

profile of v2, /device:TPU:0, one launch (start us, length us, event | category | flops | bytes accessed | tf_op | source)
XLA Modules:
  0.0 525.2 jit_solution(15329425207110998938)
XLA Ops:
  9.7 22.9 %all-gather = bf16[448,1024]{1,0:T(8,128)(2,1)S(1)} all-gather(bf16[112,1024]{1,0:T(8,128)(2,1)S(1)} %fusion.72), channel_id=2, replica_groups=mesh['y'=2,'core'=2,'z'=4,'x'=2] {'z'}, dimensions={0}, use_global_device_ids=true | all-gather | bytes 1146880 | tf_op jit(solution)/shard_map/all_gather | solution.py:228
  36.7 6.6 %collective-permute-done = bf16[4,112,512]{2,1,0:T(8,128)(2,1)S(1)} collective-permute-done((bf16[4,112,512]{2,1,0:T(8,128)(2,1)S(1)}, bf16[4,112,512]{2,1,0:T(8,128)(2,1)S(1)}, u32[]{:S(2)}, u32[]{:S(2)}) %collective-permute-start) | collective-permute-done | bytes 458784 | tf_op jit(solution)/shard_map/ppermute | solution.py:221
  51.2 10.6 %collective-permute-done.1.refs_1_ = bf16[2,4,112,512]{3,2,1,0:T(8,128)(2,1)S(1)} collective-permute-done((bf16[2,4,112,512]{3,2,1,0:T(8,128)(2,1)S(1)}, bf16[2,4,112,512]{3,2,1,0:T(8,128)(2,1)S(1)}, u32[]{:S(2)}, u32[]{:S(2)}) %collective-permute-start.1) | collective-permute-done | bytes 917536 | tf_op jit(solution)/shard_map/ppermute | solution.py:221
  61.8 2.0 collective-permute-done.3.refs_3_
  67.2 2.4 fusion.100
  72.7 5.8 %shard_map.356 = (bf16[32,32,1024]{2,1,0:T(8,128)(2,1)S(1)}, bf16[32,32,1024]{2,1,0:T(8,128)(2,1)S(1)}, bf16[32,32,1024]{2,1,0:T(8,128)(2,1)}, bf16[32,16,1024]{2,1,0:T(8,128)(2,1)S(1)}) custom-call(s32[3]{0:T(128)S(1)} %pad_add_fusion.at_ref, bf16[2,4,112,512]{3,2,1,0:T(8,128)(2,1)S(1)} %pad_maximum_fusion.15.refs_0_, ...), custom_call_target="tpu_custom_call" | custom-call | tf_op jit(solution)/shard_map/pallas_call | solution.py:279
  82.3 1.7 fusion.6
  86.8 1.9 add_convert_fusion.15
  88.8 2.6 fusion.108.r_ref
  93.5 2.7 multiply_reduce_fusion.9
  97.5 2.3 pad_maximum_fusion.3.refs_2_
  99.8 3.0 collective-permute-start.14
  103.9 1.9 collective-permute-start.11
  105.8 1.9 collective-permute-start.10
  107.7 2.2 collective-permute-start.9
  110.2 20.0 %collective-permute-done.11 = f32[2,2,1024]{2,1,0:T(2,128)} collective-permute-done((f32[2,2,1024]{2,1,0:T(2,128)}, f32[2,2,1024]{2,1,0:T(2,128)}, u32[]{:S(2)}, u32[]{:S(2)}) %collective-permute-start.11) | collective-permute-done | bytes 16416 | tf_op jit(solution)/shard_map/ppermute | solution.py:192
  136.4 4.6 shard_map.357
  144.7 2.4 fusion.99
  148.0 16.4 %collective-permute-done.21 = bf16[4,160,512]{2,1,0:T(8,128)(2,1)} collective-permute-done((bf16[4,160,512]{2,1,0:T(8,128)(2,1)}, bf16[4,160,512]{2,1,0:T(8,128)(2,1)}, u32[]{:S(2)}, u32[]{:S(2)}) %collective-permute-start.21) | collective-permute-done | bytes 655392 | tf_op jit(solution)/shard_map/ppermute | solution.py:221
  164.3 1.7 collective-permute-start.22
  166.1 2.5 pad_maximum_fusion.4.refs_0_
  168.6 8.2 %shard_map.358 = (bf16[32,32,1024]{2,1,0:T(8,128)(2,1)S(1)}, bf16[32,32,4096]{2,1,0:T(8,128)(2,1)}) custom-call(s32[3]{0:T(128)S(1)} %pad_add_fusion.at_ref, bf16[2,4,160,512]{3,2,1,0:T(8,128)(2,1)S(1)} %pad_maximum_fusion.2.refs_0_, bf16[2,4,160,512]{3,2,1,0:T(8,128)(2,1)} %collective-permute-done.14.refs_1_, ...), custom_call_target="tpu_custom_call" | custom-call | tf_op jit(solution)/shard_map/pallas_call | solution.py:279
  181.3 2.6 add_convert_fusion.13
  183.9 3.1 collective-permute-start.23
  188.1 27.7 %collective-permute-done.23.refs_1_ = bf16[2,4,160,512]{3,2,1,0:T(8,128)(2,1)} collective-permute-done((bf16[2,4,160,512]{3,2,1,0:T(8,128)(2,1)}, bf16[2,4,160,512]{3,2,1,0:T(8,128)(2,1)}, u32[]{:S(2)}, u32[]{:S(2)}) %collective-permute-start.23) | collective-permute-done | bytes 1310752 | tf_op jit(solution)/shard_map/ppermute | solution.py:221
  216.4 10.2 %multiply_convert_fusion.1 = (bf16[2,256,4096]{2,1,0:T(8,128)(2,1)S(1)}, bf16[2,256,4096]{2,1,0:T(8,128)(2,1)}) fusion(bf16[2,256,1024]{2,1,0:T(8,128)(2,1)} %get-tuple-element.185, bf16[1024,4096,1]{1,0,2:T(8,128)(2,1)} %bitcast.449), kind=kOutput, calls=%fused_computation.5 | convolution fusion | flops 4303355904 | bytes 17825792 | tf_op jit(solution)/shard_map/nlc,cf->nlf/dot_general | solution.py:186
  228.2 6.6 %shard_map.359 = (bf16[32,32,1024]{2,1,0:T(8,128)(2,1)S(1)}, bf16[32,128,1024]{2,1,0:T(8,128)(2,1)}) custom-call(s32[3]{0:T(128)S(1)} %pad_add_fusion.at_ref, bf16[2,4,160,512]{3,2,1,0:T(8,128)(2,1)} %pad_maximum_fusion.4.refs_0_, bf16[2,4,160,512]{3,2,1,0:T(8,128)(2,1)} %collective-permute-done.23.refs_1_, ...), custom_call_target="tpu_custom_call" | custom-call | tf_op jit(solution)/shard_map/pallas_call | solution.py:279
  234.8 7.6 %fusion.109 = f32[2,256,1024]{2,1,0:T(8,128)S(1)} fusion(bf16[2,256,4096]{2,1,0:T(8,128)(2,1)S(1)} %get-tuple-element.326, bf16[4096,1024,1]{1,0,2:T(8,128)(2,1)} %bitcast.451), kind=kOutput, calls=%fused_computation.388 | convolution fusion | flops 4294967296 | bytes 14680064 | tf_op jit(solution)/shard_map/nlf,fd->nld/dot_general | solution.py:186
  242.5 3.4 multiply_convert_fusion.3
  245.9 4.4 bitcast_convert_fusion.1
  250.3 2.2 broadcast_select_fusion.13
  255.6 9.1 %multiply_convert_fusion = bf16[2,256,4096]{2,1,0:T(8,128)(2,1)S(1)} fusion(bf16[2,256,4096]{2,1,0:T(8,128)(2,1)} %get-tuple-element.327, bf16[2,256,1024]{2,1,0:T(8,128)(2,1)S(1)} %copy-done.127, bf16[4096,1024,1]{1,0,2:T(8,128)(2,1)} %bitcast.452), kind=kOutput, calls=%fused_computation.4 | convolution fusion | flops 4307550208 | bytes 17825792 | tf_op jit(solution)/shard_map/nld,fd->nlf/dot_general | solution.py:186
  264.7 4.3 bitcast_convert_fusion
  276.8 5.7 %fusion.16 = f32[2048,1024,1]{1,0,2:T(8,128)} fusion(bf16[2,256,1024]{2,1,0:T(8,128)(2,1)S(1)} %copy-done.128, bf16[2,256,1024]{2,1,0:T(8,128)(2,1)S(1)} %copy-done.60, bf16[2,256,1024]{2,1,0:T(8,128)(2,1)S(1)} %copy-done.59), kind=kOutput, calls=%fused_computation.30 | convolution fusion | flops 2151677952 | bytes 11534336 | tf_op jit(solution)/shard_map/nlc,nld->cd/dot_general | solution.py:507
  282.5 6.4 %add_convert_fusion.1 = bf16[2,4,2,128,1024]{4,3,2,1,0:T(8,128)(2,1)S(1)} fusion(f32[2,4,2,128,1024]{4,3,2,1,0:T(8,128)} %bitcast.391, bf16[2,4,2,128,1024]{4,3,2,1,0:T(8,128)(2,1)} %collective-permute-done.30), kind=kLoop, calls=%fused_computation.3 | loop fusion | flops 6291456 | bytes 16777216 | tf_op jit(solution)/shard_map/convert_element_type | solution.py:515
  295.0 7.5 %fusion.110 = f32[2,256,1024]{2,1,0:T(8,128)S(1)} fusion(bf16[2,256,4096]{2,1,0:T(8,128)(2,1)S(1)} %multiply_convert_fusion, bf16[1024,4096,1]{1,0,2:T(8,128)(2,1)} %bitcast.450), kind=kOutput, calls=%fused_computation.389 | convolution fusion | flops 4294967296 | bytes 14680064 | tf_op jit(solution)/shard_map/nlf,cf->nlc/dot_general | solution.py:186
  302.5 3.1 multiply_reduce_fusion
  309.1 2.4 fusion.39
  311.6 5.6 %add_convert_fusion = bf16[2,4,2,32,4096]{4,3,2,1,0:T(8,128)(2,1)} fusion(f32[2,4,2,32,4096]{4,3,2,1,0:T(8,128)S(1)} %bitcast.383, bf16[2,4,2,32,4096]{4,3,2,1,0:T(8,128)(2,1)} %collective-permute-done.29), kind=kLoop, calls=%fused_computation.2 | loop fusion | flops 6291456 | bytes 16777216 | tf_op jit(solution)/shard_map/convert_element_type | solution.py:515
  317.2 2.7 fusion.97
  329.5 1.8 copy.140
  336.4 5.5 %multiply_reduce_fusion.2 = (f32[1024]{0:T(1024)S(1)}, f32[2,256]{1,0:T(2,128)S(1)}, f32[2,256]{1,0:T(2,128)S(1)}, f32[1024]{0:T(1024)S(1)}, f32[2,256,1024]{2,1,0:T(8,128)}) fusion(f32[2,256,1024]{2,1,0:T(8,128)S(1)} %copy-done.25, f32[2,256]{1,0:T(2,128)S(1)} %add_rsqrt_fusion, f32[2,256]{1,0:T(2,128)S(1)} %broadcast_multiply_fusion.5, f32[1024]{0:T(1024)S(1)} %mul.464, ...), kind=kLoop, calls=%fused_computation.45 | loop fusion | flops 7336960 | bytes 10514432 | tf_op jit(solution)/shard_map/reduce_sum | solution.py:544
  342.1 3.2 fusion.95
  345.4 2.1 add_convert_fusion.2
  349.2 1.9 add_convert_fusion.3
  351.1 2.3 collective-permute-start.38
  353.4 2.7 multiply_convert_fusion.2
  362.6 1.7 bitcast_convert_fusion.5
  364.3 4.3 collective-permute-done.37
  370.2 6.0 %shard_map.360 = (bf16[2,256,1024]{2,1,0:T(8,128)(2,1)S(1)}, bf16[2,256,1024]{2,1,0:T(8,128)(2,1)S(1)}, f32[1,1024]{1,0:T(1,128)S(1)}, f32[1,1024]{1,0:T(1,128)S(1)}) custom-call(f32[2,256,1024]{2,1,0:T(8,128)S(1)} %fusion.107.k_ref, f32[2,256,1024]{2,1,0:T(8,128)S(1)} %copy-done.1, f32[2,256,1024]{2,1,0:T(8,128)S(1)} %copy-done.3, ...), custom_call_target="tpu_custom_call" | custom-call | flops 26214400 | bytes 14680064 | tf_op jit(solution)/shard_map/pallas_call | solution.py:172
  381.4 2.1 fusion.52
  385.5 2.2 fusion.59
  410.9 2.7 collective-permute-done.46
  417.6 2.7 multiply_add_fusion
  427.4 7.1 %fusion.11 = (f32[1024]{0:T(1024)}, f32[2,256]{1,0:T(2,128)S(1)}, f32[2,256]{1,0:T(2,128)}, f32[1024]{0:T(1024)}, f32[1024]{0:T(1024)}, /*index=5*/f32[1024]{0:T(1024)}, f32[1024]{0:T(1024)}, f32[2,256,1024]{2,1,0:T(8,128)}) fusion(bf16[2,256,1024]{2,1,0:T(8,128)(2,1)S(1)} %copy-done.29, f32[2,256]{1,0:T(2,128)S(1)} %copy-done.114, ...), kind=kLoop, calls=%fused_computation.23 | loop fusion | flops 14149632 | bytes 13680640 | tf_op jit(solution)/shard_map/reduce_sum | solution.py:606
  444.3 19.4 %collective-permute-start.49 = (f32[2,4,2,11,32]{4,2,1,0,3:T(2,128)S(1)}, f32[2,4,2,11,32]{4,2,1,0,3:T(2,128)S(1)}, u32[]{:S(2)}, u32[]{:S(2)}) collective-permute-start(f32[2,4,2,11,32]{4,2,1,0,3:T(2,128)S(1)} %dynamic-slice_bitcast_fusion.26), channel_id=1, source_target_pairs={{0,8},{8,0},{1,9},{9,1},{2,10},{10,2},{3,11},{11,3},{4,12},{12,4},... | collective-permute-start | bytes 67592 | tf_op jit(solution)/shard_map/ppermute | solution.py:301
  463.8 4.3 fusion.10
  473.8 9.9 %collective-permute-done.56 = bf16[4,128,512]{2,1,0:T(8,128)(2,1)S(1)} collective-permute-done((bf16[4,128,512]{2,1,0:T(8,128)(2,1)S(1)}, bf16[4,128,512]{2,1,0:T(8,128)(2,1)S(1)}, u32[]{:S(2)}, u32[]{:S(2)}) %collective-permute-start.56) | collective-permute-done | bytes 524320 | tf_op jit(solution)/shard_map/ppermute | solution.py:301
  483.9 2.1 collective-permute-done.58
  487.3 1.8 collective-permute-start.51
  489.1 2.2 collective-permute-done.51
  493.0 2.7 collective-permute-start.54
  497.3 3.1 collective-permute-done.53
  505.3 11.3 %reduce-scatter.4.cloned.1.call-done = bf16[1,128,1024]{2,1,0:T(8,128)(2,1)} async-done(((bf16[4,128,1024]{2,1,0:T(8,128)(2,1)}), bf16[1,128,1024]{2,1,0:T(8,128)(2,1)}) %reduce-scatter.4.cloned.1.call-update) | async-done | bytes 262160 | tf_op jit(solution)/shard_map/reduce_scatter | solution.py:328
  (575 shorter events, 162.8 us)
Async XLA Ops:
  7.2 60.0 %all-gather.6.cloned.1.call-start = ((), (), s32[]{:S(2)}) async-start(), calls=%async_computation.6 | async-start | bytes 1638400 | tf_op jit(solution)/shard_map/all_gather | solution.py:228
  32.8 11.3 %collective-permute-start.2 = (bf16[4,112,512]{2,1,0:T(8,128)(2,1)S(1)}, bf16[4,112,512]{2,1,0:T(8,128)(2,1)S(1)}, u32[]{:S(2)}, u32[]{:S(2)}) collective-permute-start(bf16[4,112,512]{2,1,0:T(8,128)(2,1)S(1)} %get-tuple-element.252), channel_id=1, source_target_pairs={{0,16},{16,0},{1,17},{17,1},{2,18},{18,2},{3,19},{19,3},{4,20},{20... | collective-permute-start | bytes 1376264 | tf_op jit(solution)/shard_map/ppermute | solution.py:221
  34.3 9.0 %collective-permute-start = (bf16[4,112,512]{2,1,0:T(8,128)(2,1)S(1)}, bf16[4,112,512]{2,1,0:T(8,128)(2,1)S(1)}, u32[]{:S(2)}, u32[]{:S(2)}) collective-permute-start(bf16[4,112,512]{2,1,0:T(8,128)(2,1)S(1)} %get-tuple-element.253), channel_id=1, source_target_pairs={{0,1},{1,0},{2,3},{3,2},{4,5},{5,4},{6,7},{7,6},{8,9},{9,8},{10,11... | collective-permute-start | bytes 1376264 | tf_op jit(solution)/shard_map/ppermute | solution.py:221
  36.7 108.1 %all-gather.8.cloned.1.call-start = ((), (), s32[]{:S(2)}) async-start(), calls=%async_computation.7 | async-start | bytes 1638400 | tf_op jit(solution)/shard_map/all_gather | solution.py:228
  43.5 18.3 %collective-permute-start.1 = (bf16[2,4,112,512]{3,2,1,0:T(8,128)(2,1)S(1)}, bf16[2,4,112,512]{3,2,1,0:T(8,128)(2,1)S(1)}, u32[]{:S(2)}, u32[]{:S(2)}) collective-permute-start(bf16[2,4,112,512]{3,2,1,0:T(8,128)(2,1)S(1)} %pad_maximum_fusion.15.refs_0_), channel_id=1, source_target_pairs={{0,16},{16,0},{1,17},{17,1},{2,18},{18,2},{3,19},{19,3},{4,20},{20... | collective-permute-start | bytes 2752520 | tf_op jit(solution)/shard_map/ppermute | solution.py:221
  45.9 17.9 %collective-permute-start.3 = (bf16[2,4,112,512]{3,2,1,0:T(8,128)(2,1)S(1)}, bf16[2,4,112,512]{3,2,1,0:T(8,128)(2,1)}, u32[]{:S(2)}, u32[]{:S(2)}) collective-permute-start(bf16[2,4,112,512]{3,2,1,0:T(8,128)(2,1)S(1)} %pad_maximum_fusion.16.refs_2_), channel_id=1, source_target_pairs={{0,1},{1,0},{2,3},{3,2},{4,5},{5,4},{6,7},{7,6},{8,9},{9,8},{10,11... | collective-permute-start | bytes 2752520 | tf_op jit(solution)/shard_map/ppermute | solution.py:221
  50.6 20.6 %collective-permute-start.4 = (bf16[2,4,112,512]{3,2,1,0:T(8,128)(2,1)S(1)}, bf16[2,4,112,512]{3,2,1,0:T(8,128)(2,1)}, u32[]{:S(2)}, u32[]{:S(2)}) collective-permute-start(bf16[2,4,112,512]{3,2,1,0:T(8,128)(2,1)S(1)} %pad_maximum_fusion.15.refs_0_), channel_id=1, source_target_pairs={{0,8},{8,0},{1,9},{9,1},{2,10},{10,2},{3,11},{11,3},{4,12},{12,4},... | collective-permute-start | bytes 2752520 | tf_op jit(solution)/shard_map/ppermute | solution.py:221
  50.7 22.0 %collective-permute-start.6 = (bf16[2,4,112,512]{3,2,1,0:T(8,128)(2,1)S(1)}, bf16[2,4,112,512]{3,2,1,0:T(8,128)(2,1)}, u32[]{:S(2)}, u32[]{:S(2)}) collective-permute-start(bf16[2,4,112,512]{3,2,1,0:T(8,128)(2,1)S(1)} %pad_maximum_fusion.16.refs_2_), channel_id=1, source_target_pairs={{0,8},{8,0},{1,9},{9,1},{2,10},{10,2},{3,11},{11,3},{4,12},{12,4},... | collective-permute-start | bytes 2752520 | tf_op jit(solution)/shard_map/ppermute | solution.py:221
  61.8 10.9 %collective-permute-start.5 = (bf16[2,4,112,512]{3,2,1,0:T(8,128)(2,1)S(1)}, bf16[2,4,112,512]{3,2,1,0:T(8,128)(2,1)}, u32[]{:S(2)}, u32[]{:S(2)}) collective-permute-start(bf16[2,4,112,512]{3,2,1,0:T(8,128)(2,1)S(1)} %collective-permute-done.1.refs_1_), channel_id=1, source_target_pairs={{0,8},{8,0},{1,9},{9,1},{2,10},{10,2},{3,11},{11,3},{4,12},{12,4},... | collective-permute-start | bytes 2752520 | tf_op jit(solution)/shard_map/ppermute | solution.py:221
  63.8 9.0 %collective-permute-start.7 = (bf16[2,4,112,512]{3,2,1,0:T(8,128)(2,1)}, bf16[2,4,112,512]{3,2,1,0:T(8,128)(2,1)}, u32[]{:S(2)}, u32[]{:S(2)}) collective-permute-start(bf16[2,4,112,512]{3,2,1,0:T(8,128)(2,1)} %collective-permute-done.3.refs_3_), channel_id=1, source_target_pairs={{0,8},{8,0},{1,9},{9,1},{2,10},{10,2},{3,11},{11,3},{4,12},{12,4},... | collective-permute-start | bytes 2752520 | tf_op jit(solution)/shard_map/ppermute | solution.py:221
  69.7 431.3 %reduce-scatter.8.cloned.1.call-start = ((), (), s32[]{:S(2)}) async-start(), calls=%async_computation.5 | async-start | bytes 1638400 | tf_op jit(solution)/shard_map/reduce_scatter | solution.py:328
  69.7 26.5 %collective-permute-start.12 = (bf16[4,160,512]{2,1,0:T(8,128)(2,1)}, bf16[4,160,512]{2,1,0:T(8,128)(2,1)}, u32[]{:S(2)}, u32[]{:S(2)}) collective-permute-start(bf16[4,160,512]{2,1,0:T(8,128)(2,1)} %get-tuple-element.90), channel_id=1, source_target_pairs={{0,1},{1,0},{2,3},{3,2},{4,5},{5,4},{6,7},{7,6},{8,9},{9,8},{10,11... | collective-permute-start | bytes 1966088 | tf_op jit(solution)/shard_map/ppermute | solution.py:221
  71.3 26.2 %collective-permute-start.13 = (bf16[4,160,512]{2,1,0:T(8,128)(2,1)}, bf16[4,160,512]{2,1,0:T(8,128)(2,1)}, u32[]{:S(2)}, u32[]{:S(2)}) collective-permute-start(bf16[4,160,512]{2,1,0:T(8,128)(2,1)} %get-tuple-element.91), channel_id=1, source_target_pairs={{0,16},{16,0},{1,17},{17,1},{2,18},{18,2},{3,19},{19,3},{4,20},{20... | collective-permute-start | bytes 1966088 | tf_op jit(solution)/shard_map/ppermute | solution.py:221
  84.1 2.6 collective-permute-start.8
  99.8 32.1 %collective-permute-start.14 = (bf16[2,4,160,512]{3,2,1,0:T(8,128)(2,1)S(1)}, bf16[2,4,160,512]{3,2,1,0:T(8,128)(2,1)}, u32[]{:S(2)}, u32[]{:S(2)}) collective-permute-start(bf16[2,4,160,512]{3,2,1,0:T(8,128)(2,1)S(1)} %pad_maximum_fusion.2.refs_0_), channel_id=1, source_target_pairs={{0,16},{16,0},{1,17},{17,1},{2,18},{18,2},{3,19},{19,3},{4,20},{20... | collective-permute-start | bytes 3932168 | tf_op jit(solution)/shard_map/ppermute | solution.py:221
  102.8 29.4 %collective-permute-start.15 = (bf16[2,4,160,512]{3,2,1,0:T(8,128)(2,1)}, bf16[2,4,160,512]{3,2,1,0:T(8,128)(2,1)}, u32[]{:S(2)}, u32[]{:S(2)}) collective-permute-start(bf16[2,4,160,512]{3,2,1,0:T(8,128)(2,1)} %pad_maximum_fusion.3.refs_2_), channel_id=1, source_target_pairs={{0,1},{1,0},{2,3},{3,2},{4,5},{5,4},{6,7},{7,6},{8,9},{9,8},{10,11... | collective-permute-start | bytes 3932168 | tf_op jit(solution)/shard_map/ppermute | solution.py:221
  103.9 26.2 %collective-permute-start.11 = (f32[2,2,1024]{2,1,0:T(2,128)}, f32[2,2,1024]{2,1,0:T(2,128)}, u32[]{:S(2)}, u32[]{:S(2)}) collective-permute-start(f32[2,2,1024]{2,1,0:T(2,128)} %pad_maximum_fusion.19), channel_id=1, source_target_pairs={{0,24},{1,25},{2,26},{3,27},{4,28},{5,29},{6,30},{7,31}} | collective-permute-start | bytes 49160 | tf_op jit(solution)/shard_map/ppermute | solution.py:192
  105.8 24.5 %collective-permute-start.10 = (f32[2,2,1024]{2,1,0:T(2,128)}, f32[2,2,1024]{2,1,0:T(2,128)}, u32[]{:S(2)}, u32[]{:S(2)}) collective-permute-start(f32[2,2,1024]{2,1,0:T(2,128)} %pad_maximum_fusion.19), channel_id=1, source_target_pairs={{0,16},{8,24},{1,17},{9,25},{2,18},{10,26},{3,19},{11,27},{4,20},{... | collective-permute-start | bytes 49160 | tf_op jit(solution)/shard_map/ppermute | solution.py:192
  107.7 24.7 %collective-permute-start.9 = (f32[2,2,1024]{2,1,0:T(2,128)}, f32[2,2,1024]{2,1,0:T(2,128)}, u32[]{:S(2)}, u32[]{:S(2)}) collective-permute-start(f32[2,2,1024]{2,1,0:T(2,128)} %pad_maximum_fusion.19), channel_id=1, source_target_pairs={{0,8},{8,16},{16,24},{1,9},{9,17},{17,25},{2,10},{10,18},{18,26},{... | collective-permute-start | bytes 49160 | tf_op jit(solution)/shard_map/ppermute | solution.py:192
  130.1 38.4 %collective-permute-start.16 = (bf16[2,4,160,512]{3,2,1,0:T(8,128)(2,1)S(1)}, bf16[2,4,160,512]{3,2,1,0:T(8,128)(2,1)}, u32[]{:S(2)}, u32[]{:S(2)}) collective-permute-start(bf16[2,4,160,512]{3,2,1,0:T(8,128)(2,1)S(1)} %pad_maximum_fusion.2.refs_0_), channel_id=1, source_target_pairs={{0,8},{8,0},{1,9},{9,1},{2,10},{10,2},{3,11},{11,3},{4,12},{12,4},... | collective-permute-start | bytes 3932168 | tf_op jit(solution)/shard_map/ppermute | solution.py:221
  130.3 38.3 %collective-permute-start.18 = (bf16[2,4,160,512]{3,2,1,0:T(8,128)(2,1)}, bf16[2,4,160,512]{3,2,1,0:T(8,128)(2,1)}, u32[]{:S(2)}, u32[]{:S(2)}) collective-permute-start(bf16[2,4,160,512]{3,2,1,0:T(8,128)(2,1)} %pad_maximum_fusion.3.refs_2_), channel_id=1, source_target_pairs={{0,8},{8,0},{1,9},{9,1},{2,10},{10,2},{3,11},{11,3},{4,12},{12,4},... | collective-permute-start | bytes 3932168 | tf_op jit(solution)/shard_map/ppermute | solution.py:221
  131.9 36.7 %collective-permute-start.17 = (bf16[2,4,160,512]{3,2,1,0:T(8,128)(2,1)}, bf16[2,4,160,512]{3,2,1,0:T(8,128)(2,1)}, u32[]{:S(2)}, u32[]{:S(2)}) collective-permute-start(bf16[2,4,160,512]{3,2,1,0:T(8,128)(2,1)} %collective-permute-done.14.refs_1_), channel_id=1, source_target_pairs={{0,8},{8,0},{1,9},{9,1},{2,10},{10,2},{3,11},{11,3},{4,12},{12,4},... | collective-permute-start | bytes 3932168 | tf_op jit(solution)/shard_map/ppermute | solution.py:221
  132.1 36.5 %collective-permute-start.19 = (bf16[2,4,160,512]{3,2,1,0:T(8,128)(2,1)}, bf16[2,4,160,512]{3,2,1,0:T(8,128)(2,1)}, u32[]{:S(2)}, u32[]{:S(2)}) collective-permute-start(bf16[2,4,160,512]{3,2,1,0:T(8,128)(2,1)} %collective-permute-done.15.refs_3_), channel_id=1, source_target_pairs={{0,8},{8,0},{1,9},{9,1},{2,10},{10,2},{3,11},{11,3},{4,12},{12,4},... | collective-permute-start | bytes 3932168 | tf_op jit(solution)/shard_map/ppermute | solution.py:221
  147.2 17.2 %collective-permute-start.21 = (bf16[4,160,512]{2,1,0:T(8,128)(2,1)}, bf16[4,160,512]{2,1,0:T(8,128)(2,1)}, u32[]{:S(2)}, u32[]{:S(2)}) collective-permute-start(bf16[4,160,512]{2,1,0:T(8,128)(2,1)} %get-tuple-element.96), channel_id=1, source_target_pairs={{0,1},{1,0},{2,3},{3,2},{4,5},{5,4},{6,7},{7,6},{8,9},{9,8},{10,11... | collective-permute-start | bytes 1966088 | tf_op jit(solution)/shard_map/ppermute | solution.py:221
  164.3 16.6 %collective-permute-start.22 = (bf16[4,160,512]{2,1,0:T(8,128)(2,1)}, bf16[4,160,512]{2,1,0:T(8,128)(2,1)S(1)}, u32[]{:S(2)}, u32[]{:S(2)}) collective-permute-start(bf16[4,160,512]{2,1,0:T(8,128)(2,1)} %get-tuple-element.97), channel_id=1, source_target_pairs={{0,16},{16,0},{1,17},{17,1},{2,18},{18,2},{3,19},{19,3},{4,20},{20... | collective-permute-start | bytes 1966088 | tf_op jit(solution)/shard_map/ppermute | solution.py:221
  179.0 2.3 collective-permute-start.20
  183.9 31.9 %collective-permute-start.23 = (bf16[2,4,160,512]{3,2,1,0:T(8,128)(2,1)}, bf16[2,4,160,512]{3,2,1,0:T(8,128)(2,1)}, u32[]{:S(2)}, u32[]{:S(2)}) collective-permute-start(bf16[2,4,160,512]{3,2,1,0:T(8,128)(2,1)} %pad_maximum_fusion.4.refs_0_), channel_id=1, source_target_pairs={{0,16},{16,0},{1,17},{17,1},{2,18},{18,2},{3,19},{19,3},{4,20},{20... | collective-permute-start | bytes 3932168 | tf_op jit(solution)/shard_map/ppermute | solution.py:221
  187.0 28.8 %collective-permute-start.24 = (bf16[2,4,160,512]{3,2,1,0:T(8,128)(2,1)S(1)}, bf16[2,4,160,512]{3,2,1,0:T(8,128)(2,1)}, u32[]{:S(2)}, u32[]{:S(2)}) collective-permute-start(bf16[2,4,160,512]{3,2,1,0:T(8,128)(2,1)S(1)} %pad_maximum_fusion.5.refs_2_), channel_id=1, source_target_pairs={{0,1},{1,0},{2,3},{3,2},{4,5},{5,4},{6,7},{7,6},{8,9},{9,8},{10,11... | collective-permute-start | bytes 3932168 | tf_op jit(solution)/shard_map/ppermute | solution.py:221
  187.6 40.5 %collective-permute-start.25 = (bf16[2,4,160,512]{3,2,1,0:T(8,128)(2,1)}, bf16[2,4,160,512]{3,2,1,0:T(8,128)(2,1)S(1)}, u32[]{:S(2)}, u32[]{:S(2)}) collective-permute-start(bf16[2,4,160,512]{3,2,1,0:T(8,128)(2,1)} %pad_maximum_fusion.4.refs_0_), channel_id=1, source_target_pairs={{0,8},{8,0},{1,9},{9,1},{2,10},{10,2},{3,11},{11,3},{4,12},{12,4},... | collective-permute-start | bytes 3932168 | tf_op jit(solution)/shard_map/ppermute | solution.py:221
  187.6 40.5 %collective-permute-start.27 = (bf16[2,4,160,512]{3,2,1,0:T(8,128)(2,1)S(1)}, bf16[2,4,160,512]{3,2,1,0:T(8,128)(2,1)S(1)}, u32[]{:S(2)}, u32[]{:S(2)}) collective-permute-start(bf16[2,4,160,512]{3,2,1,0:T(8,128)(2,1)S(1)} %pad_maximum_fusion.5.refs_2_), channel_id=1, source_target_pairs={{0,8},{8,0},{1,9},{9,1},{2,10},{10,2},{3,11},{11,3},{4,12},{12,4},... | collective-permute-start | bytes 3932168 | tf_op jit(solution)/shard_map/ppermute | solution.py:221
  215.8 12.3 %collective-permute-start.26 = (bf16[2,4,160,512]{3,2,1,0:T(8,128)(2,1)}, bf16[2,4,160,512]{3,2,1,0:T(8,128)(2,1)S(1)}, u32[]{:S(2)}, u32[]{:S(2)}) collective-permute-start(bf16[2,4,160,512]{3,2,1,0:T(8,128)(2,1)} %collective-permute-done.23.refs_1_), channel_id=1, source_target_pairs={{0,8},{8,0},{1,9},{9,1},{2,10},{10,2},{3,11},{11,3},{4,12},{12,4},... | collective-permute-start | bytes 3932168 | tf_op jit(solution)/shard_map/ppermute | solution.py:221
  215.8 12.3 %collective-permute-start.28 = (bf16[2,4,160,512]{3,2,1,0:T(8,128)(2,1)}, bf16[2,4,160,512]{3,2,1,0:T(8,128)(2,1)S(1)}, u32[]{:S(2)}, u32[]{:S(2)}) collective-permute-start(bf16[2,4,160,512]{3,2,1,0:T(8,128)(2,1)} %collective-permute-done.24.refs_3_), channel_id=1, source_target_pairs={{0,8},{8,0},{1,9},{9,1},{2,10},{10,2},{3,11},{11,3},{4,12},{12,4},... | collective-permute-start | bytes 3932168 | tf_op jit(solution)/shard_map/ppermute | solution.py:221
  250.3 23.4 %collective-permute-start.30 = (bf16[2,4,2,128,1024]{4,3,2,1,0:T(8,128)(2,1)}, bf16[2,4,2,128,1024]{4,3,2,1,0:T(8,128)(2,1)}, u32[]{:S(2)}, u32[]{:S(2)}) collective-permute-start(bf16[2,4,2,128,1024]{4,3,2,1,0:T(8,128)(2,1)} %bitcast.51), channel_id=1, source_target_pairs={{0,8},{8,0},{1,9},{9,1},{2,10},{10,2},{3,11},{11,3},{4,12},{12,4},... | collective-permute-start | bytes 12582920 | tf_op jit(solution)/shard_map/ppermute | solution.py:221
  255.1 18.7 %collective-permute-start.31 = (bf16[2,4,2,32,1024]{4,3,2,1,0:T(8,128)(2,1)}, bf16[2,4,2,32,1024]{4,3,2,1,0:T(8,128)(2,1)S(1)}, u32[]{:S(2)}, u32[]{:S(2)}) collective-permute-start(bf16[2,4,2,32,1024]{4,3,2,1,0:T(8,128)(2,1)} %bitcast.53), channel_id=1, source_target_pairs={{0,8},{8,0},{1,9},{9,1},{2,10},{10,2},{3,11},{11,3},{4,12},{12,4},... | collective-permute-start | bytes 3145736 | tf_op jit(solution)/shard_map/ppermute | solution.py:221
  269.0 25.9 %collective-permute-start.29 = (bf16[2,4,2,32,4096]{4,3,2,1,0:T(8,128)(2,1)}, bf16[2,4,2,32,4096]{4,3,2,1,0:T(8,128)(2,1)}, u32[]{:S(2)}, u32[]{:S(2)}) collective-permute-start(bf16[2,4,2,32,4096]{4,3,2,1,0:T(8,128)(2,1)} %bitcast.56), channel_id=1, source_target_pairs={{0,8},{8,0},{1,9},{9,1},{2,10},{10,2},{3,11},{11,3},{4,12},{12,4},... | collective-permute-start | bytes 12582920 | tf_op jit(solution)/shard_map/ppermute | solution.py:221
  290.9 54.5 %collective-permute-start.34 = (bf16[4,2,160,512]{3,2,0,1:T(8,128)(2,1)}, bf16[4,2,160,512]{3,2,0,1:T(8,128)(2,1)}, u32[]{:S(2)}, u32[]{:S(2)}) collective-permute-start(bf16[4,2,160,512]{3,2,0,1:T(8,128)(2,1)} %pad_maximum_fusion.7), channel_id=1, source_target_pairs={{0,16},{16,0},{1,17},{17,1},{2,18},{18,2},{3,19},{19,3},{4,20},{20... | collective-permute-start | bytes 3932168 | tf_op jit(solution)/shard_map/ppermute | solution.py:301
  307.3 41.9 %collective-permute-start.33 = (bf16[2,4,160,512]{3,2,1,0:T(8,128)(2,1)}, bf16[2,4,160,512]{3,2,1,0:T(8,128)(2,1)}, u32[]{:S(2)}, u32[]{:S(2)}) collective-permute-start(bf16[2,4,160,512]{3,2,1,0:T(8,128)(2,1)} %pad_maximum_fusion.6), channel_id=1, source_target_pairs={{0,1},{1,0},{2,3},{3,2},{4,5},{5,4},{6,7},{7,6},{8,9},{9,8},{10,11... | collective-permute-start | bytes 3932168 | tf_op jit(solution)/shard_map/ppermute | solution.py:301
  307.8 28.6 %collective-permute-start.32 = (f32[2,1024]{1,0:T(2,128)S(1)}, f32[2,1024]{1,0:T(2,128)S(1)}, u32[]{:S(2)}, u32[]{:S(2)}) collective-permute-start(f32[2,1024]{1,0:T(2,128)S(1)} %bitcast.430), channel_id=1, source_target_pairs={{8,0},{16,8},{24,16},{9,1},{17,9},{25,17},{10,2},{18,10},{26,18},{... | collective-permute-start | bytes 24584 | tf_op jit(solution)/shard_map/ppermute | solution.py:192
  347.6 21.7 %collective-permute-start.39 = (bf16[4,160,512]{2,1,0:T(8,128)(2,1)S(1)}, bf16[4,160,512]{2,1,0:T(8,128)(2,1)S(1)}, u32[]{:S(2)}, u32[]{:S(2)}) collective-permute-start(bf16[4,160,512]{2,1,0:T(8,128)(2,1)S(1)} %dynamic-slice_bitcast_fusion.2), channel_id=1, source_target_pairs={{0,1},{1,0},{2,3},{3,2},{4,5},{5,4},{6,7},{7,6},{8,9},{9,8},{10,11... | collective-permute-start | bytes 1966088 | tf_op jit(solution)/shard_map/ppermute | solution.py:301
  351.1 18.1 %collective-permute-start.38 = (bf16[4,160,512]{2,1,0:T(8,128)(2,1)S(1)}, bf16[4,160,512]{2,1,0:T(8,128)(2,1)S(1)}, u32[]{:S(2)}, u32[]{:S(2)}) collective-permute-start(bf16[4,160,512]{2,1,0:T(8,128)(2,1)S(1)} %dynamic-slice_bitcast_fusion.3), channel_id=1, source_target_pairs={{0,16},{16,0},{1,17},{17,1},{2,18},{18,2},{3,19},{19,3},{4,20},{20... | collective-permute-start | bytes 1966088 | tf_op jit(solution)/shard_map/ppermute | solution.py:301
  356.7 12.0 %collective-permute-start.37 = (f32[2,2,1024]{2,1,0:T(2,128)S(1)}, f32[2,2,1024]{2,1,0:T(2,128)S(1)}, u32[]{:S(2)}, u32[]{:S(2)}) collective-permute-start(f32[2,2,1024]{2,1,0:T(2,128)S(1)} %pad_maximum_fusion.20), channel_id=1, source_target_pairs={{24,0},{25,1},{26,2},{27,3},{28,4},{29,5},{30,6},{31,7}} | collective-permute-start | bytes 49160 | tf_op jit(solution)/shard_map/ppermute | solution.py:192
  358.1 11.1 %collective-permute-start.36 = (f32[2,2,1024]{2,1,0:T(2,128)S(1)}, f32[2,2,1024]{2,1,0:T(2,128)S(1)}, u32[]{:S(2)}, u32[]{:S(2)}) collective-permute-start(f32[2,2,1024]{2,1,0:T(2,128)S(1)} %pad_maximum_fusion.20), channel_id=1, source_target_pairs={{16,0},{24,8},{17,1},{25,9},{18,2},{26,10},{19,3},{27,11},{20,4},{... | collective-permute-start | bytes 49160 | tf_op jit(solution)/shard_map/ppermute | solution.py:192
  359.4 9.8 %collective-permute-start.35 = (f32[2,2,1024]{2,1,0:T(2,128)S(1)}, f32[2,2,1024]{2,1,0:T(2,128)S(1)}, u32[]{:S(2)}, u32[]{:S(2)}) collective-permute-start(f32[2,2,1024]{2,1,0:T(2,128)S(1)} %pad_maximum_fusion.20), channel_id=1, source_target_pairs={{8,0},{16,8},{24,16},{9,1},{17,9},{25,17},{10,2},{18,10},{26,18},{... | collective-permute-start | bytes 49160 | tf_op jit(solution)/shard_map/ppermute | solution.py:192
  368.7 19.1 %collective-permute-start.43 = (bf16[2,4,2,32,1024]{4,3,2,1,0:T(8,128)(2,1)}, bf16[2,4,2,32,1024]{4,3,2,1,0:T(8,128)(2,1)}, u32[]{:S(2)}, u32[]{:S(2)}) collective-permute-start(bf16[2,4,2,32,1024]{4,3,2,1,0:T(8,128)(2,1)} %bitcast.103), channel_id=1, source_target_pairs={{0,8},{8,0},{1,9},{9,1},{2,10},{10,2},{3,11},{11,3},{4,12},{12,4},... | collective-permute-start | bytes 3145736 | tf_op jit(solution)/shard_map/ppermute | solution.py:221
  369.2 21.7 %collective-permute-start.44 = (bf16[2,4,2,32,1024]{4,3,2,1,0:T(8,128)(2,1)}, bf16[2,4,2,32,1024]{4,3,2,1,0:T(8,128)(2,1)}, u32[]{:S(2)}, u32[]{:S(2)}) collective-permute-start(bf16[2,4,2,32,1024]{4,3,2,1,0:T(8,128)(2,1)} %bitcast.91), channel_id=1, source_target_pairs={{0,8},{8,0},{1,9},{9,1},{2,10},{10,2},{3,11},{11,3},{4,12},{12,4},... | collective-permute-start | bytes 3145736 | tf_op jit(solution)/shard_map/ppermute | solution.py:221
  369.2 26.2 %collective-permute-start.42 = (bf16[2,4,128,512]{3,2,1,0:T(8,128)(2,1)}, bf16[2,4,128,512]{3,2,1,0:T(8,128)(2,1)}, u32[]{:S(2)}, u32[]{:S(2)}) collective-permute-start(bf16[2,4,128,512]{3,2,1,0:T(8,128)(2,1)} %pad_maximum_fusion.9), channel_id=1, source_target_pairs={{0,1},{1,0},{2,3},{3,2},{4,5},{5,4},{6,7},{7,6},{8,9},{9,8},{10,11... | collective-permute-start | bytes 3145736 | tf_op jit(solution)/shard_map/ppermute | solution.py:301
  369.8 25.6 %collective-permute-start.45 = (bf16[4,2,128,512]{3,2,0,1:T(8,128)(2,1)}, bf16[4,2,128,512]{3,2,0,1:T(8,128)(2,1)}, u32[]{:S(2)}, u32[]{:S(2)}) collective-permute-start(bf16[4,2,128,512]{3,2,0,1:T(8,128)(2,1)} %pad_maximum_fusion.10), channel_id=1, source_target_pairs={{0,16},{16,0},{1,17},{17,1},{2,18},{18,2},{3,19},{19,3},{4,20},{20... | collective-permute-start | bytes 3145736 | tf_op jit(solution)/shard_map/ppermute | solution.py:301
  379.7 22.0 %collective-permute-start.41 = (bf16[2,4,2,32,1024]{4,3,2,1,0:T(8,128)(2,1)}, bf16[2,4,2,32,1024]{4,3,2,1,0:T(8,128)(2,1)}, u32[]{:S(2)}, u32[]{:S(2)}) collective-permute-start(bf16[2,4,2,32,1024]{4,3,2,1,0:T(8,128)(2,1)} %bitcast.95), channel_id=1, source_target_pairs={{0,8},{8,0},{1,9},{9,1},{2,10},{10,2},{3,11},{11,3},{4,12},{12,4},... | collective-permute-start | bytes 3145736 | tf_op jit(solution)/shard_map/ppermute | solution.py:221
  381.4 122.1 %reduce-scatter.6.cloned.1.call-start = ((), (), s32[]{:S(2)}) async-start(), calls=%async_computation.4 | async-start | bytes 1310720 | tf_op jit(solution)/shard_map/reduce_scatter | solution.py:328
  387.8 14.0 %collective-permute-start.40 = (bf16[2,4,2,32,1024]{4,3,2,1,0:T(8,128)(2,1)S(1)}, bf16[2,4,2,32,1024]{4,3,2,1,0:T(8,128)(2,1)S(1)}, u32[]{:S(2)}, u32[]{:S(2)}) collective-permute-start(bf16[2,4,2,32,1024]{4,3,2,1,0:T(8,128)(2,1)S(1)} %bitcast.453), channel_id=1, source_target_pairs={{0,8},{8,0},{1,9},{9,1},{2,10},{10,2},{3,11},{11,3},{4,12},{12,4},... | collective-permute-start | bytes 3145736 | tf_op jit(solution)/shard_map/ppermute | solution.py:221
  397.2 13.8 %collective-permute-start.47 = (bf16[4,128,512]{2,1,0:T(8,128)(2,1)S(1)}, bf16[4,128,512]{2,1,0:T(8,128)(2,1)S(1)}, u32[]{:S(2)}, u32[]{:S(2)}) collective-permute-start(bf16[4,128,512]{2,1,0:T(8,128)(2,1)S(1)} %dynamic-slice_bitcast_fusion.6), channel_id=1, source_target_pairs={{0,1},{1,0},{2,3},{3,2},{4,5},{5,4},{6,7},{7,6},{8,9},{9,8},{10,11... | collective-permute-start | bytes 1572872 | tf_op jit(solution)/shard_map/ppermute | solution.py:301
  400.5 13.2 %collective-permute-start.46 = (bf16[4,128,512]{2,1,0:T(8,128)(2,1)S(1)}, bf16[4,128,512]{2,1,0:T(8,128)(2,1)S(1)}, u32[]{:S(2)}, u32[]{:S(2)}) collective-permute-start(bf16[4,128,512]{2,1,0:T(8,128)(2,1)S(1)} %dynamic-slice_bitcast_fusion.7), channel_id=1, source_target_pairs={{0,16},{16,0},{1,17},{17,1},{2,18},{18,2},{3,19},{19,3},{4,20},{20... | collective-permute-start | bytes 1572872 | tf_op jit(solution)/shard_map/ppermute | solution.py:301
  421.9 46.2 %collective-permute-start.55 = (bf16[2,4,128,512]{3,2,1,0:T(8,128)(2,1)}, bf16[2,4,128,512]{3,2,1,0:T(8,128)(2,1)}, u32[]{:S(2)}, u32[]{:S(2)}) collective-permute-start(bf16[2,4,128,512]{3,2,1,0:T(8,128)(2,1)} %pad_maximum_fusion.11), channel_id=1, source_target_pairs={{0,1},{1,0},{2,3},{3,2},{4,5},{5,4},{6,7},{7,6},{8,9},{9,8},{10,11... | collective-permute-start | bytes 3145736 | tf_op jit(solution)/shard_map/ppermute | solution.py:301
  422.4 47.5 %collective-permute-start.57 = (bf16[4,2,128,512]{3,2,0,1:T(8,128)(2,1)}, bf16[4,2,128,512]{3,2,0,1:T(8,128)(2,1)}, u32[]{:S(2)}, u32[]{:S(2)}) collective-permute-start(bf16[4,2,128,512]{3,2,0,1:T(8,128)(2,1)} %pad_maximum_fusion.12), channel_id=1, source_target_pairs={{0,16},{16,0},{1,17},{17,1},{2,18},{18,2},{3,19},{19,3},{4,20},{20... | collective-permute-start | bytes 3145736 | tf_op jit(solution)/shard_map/ppermute | solution.py:301
  424.1 3.2 collective-permute-start.48
  427.0 89.6 %reduce-scatter.4.cloned.1.call-start = ((), (), s32[]{:S(2)}) async-start(), calls=%async_computation.3 | async-start | bytes 1310720 | tf_op jit(solution)/shard_map/reduce_scatter | solution.py:328
  444.3 28.7 %collective-permute-start.49 = (f32[2,4,2,11,32]{4,2,1,0,3:T(2,128)S(1)}, f32[2,4,2,11,32]{4,2,1,0,3:T(2,128)S(1)}, u32[]{:S(2)}, u32[]{:S(2)}) collective-permute-start(f32[2,4,2,11,32]{4,2,1,0,3:T(2,128)S(1)} %dynamic-slice_bitcast_fusion.26), channel_id=1, source_target_pairs={{0,8},{8,0},{1,9},{9,1},{2,10},{10,2},{3,11},{11,3},{4,12},{12,4},... | collective-permute-start | bytes 67592 | tf_op jit(solution)/shard_map/ppermute | solution.py:301
  469.8 13.9 %collective-permute-start.56 = (bf16[4,128,512]{2,1,0:T(8,128)(2,1)S(1)}, bf16[4,128,512]{2,1,0:T(8,128)(2,1)S(1)}, u32[]{:S(2)}, u32[]{:S(2)}) collective-permute-start(bf16[4,128,512]{2,1,0:T(8,128)(2,1)S(1)} %dynamic-slice_bitcast_fusion.5), channel_id=1, source_target_pairs={{0,16},{16,0},{1,17},{17,1},{2,18},{18,2},{3,19},{19,3},{4,20},{20... | collective-permute-start | bytes 1572872 | tf_op jit(solution)/shard_map/ppermute | solution.py:301
  471.5 14.4 %collective-permute-start.58 = (bf16[4,128,512]{2,1,0:T(8,128)(2,1)S(1)}, bf16[4,128,512]{2,1,0:T(8,128)(2,1)S(1)}, u32[]{:S(2)}, u32[]{:S(2)}) collective-permute-start(bf16[4,128,512]{2,1,0:T(8,128)(2,1)S(1)} %dynamic-slice_bitcast_fusion.4), channel_id=1, source_target_pairs={{0,1},{1,0},{2,3},{3,2},{4,5},{5,4},{6,7},{7,6},{8,9},{9,8},{10,11... | collective-permute-start | bytes 1572872 | tf_op jit(solution)/shard_map/ppermute | solution.py:301
  473.1 14.1 %collective-permute-start.50 = (f32[2,4,11,32]{3,1,0,2:T(4,128)S(1)}, f32[2,4,11,32]{3,1,0,2:T(4,128)S(1)}, u32[]{:S(2)}, u32[]{:S(2)}) collective-permute-start(f32[2,4,11,32]{3,1,0,2:T(4,128)S(1)} %bitcast.425), channel_id=1, source_target_pairs={{0,1},{1,0},{2,3},{3,2},{4,5},{5,4},{6,7},{7,6},{8,9},{9,8},{10,11... | collective-permute-start | bytes 33800 | tf_op jit(solution)/shard_map/ppermute | solution.py:301
  487.3 4.0 collective-permute-start.51
  491.3 5.9 %collective-permute-start.52 = (f32[11,32]{1,0:T(8,128)S(1)}, f32[11,32]{1,0:T(8,128)S(1)}, u32[]{:S(2)}, u32[]{:S(2)}) collective-permute-start(f32[11,32]{1,0:T(8,128)S(1)} %get-tuple-element.303), channel_id=1, source_target_pairs={{0,2},{2,4},{4,6},{6,0},{1,3},{3,5},{5,7},{7,1},{8,10},{10,12},{12... | collective-permute-start | bytes 4232 | tf_op jit(solution)/shard_map/ppermute | solution.py:301
  493.0 4.2 collective-permute-start.54
  495.7 4.7 collective-permute-start.53
  (129 other events, 772.9 us)
Sparse Core Ops, SparseCore 0:
  36.8 30.3 all-gather.5
  69.8 34.5 all-gather.7
  381.5 33.2 reduce-scatter.7
  427.1 28.8 reduce-scatter.5
  487.4 29.1 reduce-scatter.3
